TPU v7x, 256 devices: a whole 4x4x8 slice. The times are simulated.
256 devices in a mesh: gx: 4 (over x), gy: 16 (over z, y_lo), gz: 4 (over y_hi, core).
Axes of the slice: x: 4, y: 4 (y_hi: 2, y_lo: 2; y = y_hi * 2 + y_lo), z: 8, core: 2. Of those that a mesh axis runs over, the one named last changes fastest.
Arguments:
- adjoint_state: float32 [8, 16, 8, 125, 128], P('gx', 'gy', 'gz'), may hold values from -6 to 6
- bulk_modulus: float32 [8, 16, 8], P('gx', 'gy', 'gz'), may hold values from 0.5 to 2
- buoyancy: float32 [8, 16, 8], P('gx', 'gy', 'gz'), may hold values from 0.5 to 2
- water_layers: int32 [8, 16], P('gx', 'gy'), may hold values from 1 to 8
- surface_cell: int32 [8, 16], P('gx', 'gy'), may hold values from 0 to 511, as said below
Outputs:
- adjoint_state_out: float32 [8, 16, 8, 125, 128], P('gx', 'gy', 'gz')
- seafloor_trace: float32 [512, 25, 128], P(('gx', 'gy'))
Inputs may be any that keep to these rules, and one draw needn't show every extreme that they name: `surface_cell`: the owner of cell c is c // 8 along gx+gy (flat index, gx slowest). The seafloor faces of the 2 x 1 element columns of one device name only owners at flat offsets 0 to 3 from that device's own flat index, taken modulo the number of owners; each owner that is named is named exactly 2 times by that device.
All inputs are finite; a program needn't handle non-finite values.
Results may differ from a plain program's by a relative error of at most 0.0001.
Values sent between devices are 32-bit elements; how exact they have to be, the bound alone decides.
A program may use at most 64 MiB of HBM per device.

v0:
```python
import math

import jax
import jax.numpy as jnp
import numpy as np
from jax import lax
from jax.experimental import pallas as pl
from jax.experimental.pallas import tpu as pltpu
from jax.sharding import PartitionSpec as P

N_GX = 4
N_GZ = 4
N_ZC = 8
SECTIONS = 8
S_DEV = 8
GRAVITY = 2.0
DT = 0.02
MESH = pl.DeviceIdType.MESH


def derivative_rows():
    points = np.array([-1.0, -math.sqrt(3.0 / 7.0), 0.0, math.sqrt(3.0 / 7.0), 1.0])
    scales = np.array(
        [np.prod([points[a] - points[b] for b in range(5) if b != a]) for a in range(5)]
    )
    table = np.zeros((5, 5))
    for a in range(5):
        for b in range(5):
            if a != b:
                table[a, b] = scales[a] / scales[b] / (points[a] - points[b])
        table[a, a] = -np.sum(table[a])
    table[0, 0] += 5.0
    table[4, 4] -= 5.0
    table[np.abs(table) < 1e-12] = 0.0
    return table


TABLE = derivative_rows()


def weighted(row, parts):
    total = None
    for weight, part in zip(row, parts):
        if weight != 0.0:
            term = float(weight) * part
            total = term if total is None else total + term
    return total


def bit_mask(shape, bit):
    lanes = lax.broadcasted_iota(jnp.int32, shape, len(shape) - 1)
    return (lanes & (1 << bit)) != 0


def lane_roll(value, shift):
    return pltpu.roll(value, shift % 128, axis=value.ndim - 1)


def swap_pair(low, high, bit):
    width = 1 << bit
    mask = bit_mask(low.shape, bit)
    return (
        jnp.where(mask, lane_roll(high, width), low),
        jnp.where(mask, high, lane_roll(low, -width)),
    )


def swap_bits(blocks, pairs):
    blocks = list(blocks)
    for index_bit, lane_bit in pairs:
        step = 1 << index_bit
        for at in range(len(blocks)):
            if not at & step:
                blocks[at], blocks[at + step] = swap_pair(blocks[at], blocks[at + step], lane_bit)
    return blocks


def flip(value, bit):
    width = 1 << bit
    mask = bit_mask(value.shape, bit)
    return jnp.where(mask, lane_roll(value, width), lane_roll(value, -width))


def fold_pair(low, high, bit):
    mask = bit_mask(low.shape, bit)
    return jnp.where(mask, high, low) + flip(jnp.where(mask, low, high), bit)


def fold_bits(blocks, bits):
    for bit in bits:
        blocks = [fold_pair(blocks[at], blocks[at + 1], bit) for at in range(0, len(blocks), 2)]
    return blocks[0]


FIELD_BITS = ((0, 5), (1, 6))
RANK_BITS = ((0, 2), (1, 3), (2, 4))

VOL_B, VOL_K, VOL_G, ACTIVE, COL_D = 0, 1, 2, 3, 4
INNER = 9
OUTER = 21
Z_ROWS = 37
SELECT = 45
BULK, BUOY, SPEED = 46, 47, 48
N_COEF = 49


def face_of(direction):
    axis, side = direction // 2, direction % 2
    bit = 6 if axis == 0 else 4
    width = 1 << bit
    return axis, side, bit, (width if side == 1 else -width)


def kernel(
    state_hbm, bulk, buoy, layers, cells, out_hbm, trace_hbm,
    staged, nat, pack_out, pack_in, back_out, back_in, state, base, update, rate, coef,
    face_out, face_in, floor, tr_out, tr_in, tb_out, tb_in, trace,
    local_sem, a_send, a_recv, h_send, h_recv, t_send, t_recv, b_send, b_recv, c_send, c_recv,
):
    gx = lax.axis_index("gx")
    gy = lax.axis_index("gy")
    gz = lax.axis_index("gz")
    zc, y_lo = gy // 2, gy % 2
    y_hi, core = gz // 2, gz % 2
    me = y_lo * 4 + y_hi * 2 + core

    load = pltpu.make_async_copy(state_hbm, staged, local_sem.at[0])
    load.start()

    def partner(delta):
        to_y = 1 - y_lo if delta & 4 else y_lo
        to_h = 1 - y_hi if delta & 2 else y_hi
        to_c = 1 - core if delta & 1 else core
        return (gx, zc * 2 + to_y, to_h * 2 + to_c), to_y * 4 + to_h * 2 + to_c, to_y

    def along(steps):
        flat = (gx * N_ZC + zc + steps + N_GX * N_ZC) % (N_GX * N_ZC)
        return (flat // N_ZC, (flat % N_ZC) * 2 + y_lo, gz)

    neighbours = [
        ((gx + N_GX - 1) % N_GX, gy, gz),
        ((gx + 1) % N_GX, gy, gz),
        (gx, (gy + 2 * N_ZC - 2) % (2 * N_ZC), gz),
        (gx, (gy + 2) % (2 * N_ZC), gz),
    ]
    barrier = pltpu.get_barrier_semaphore()
    greeted = [partner(delta)[0] for delta in range(1, 8)] + neighbours
    greeted += [along(steps) for steps in (1, 2, -1, -2)]
    for device in greeted:
        pl.semaphore_signal(barrier, inc=1, device_id=device, device_id_type=MESH)

    floor[...] = jnp.zeros_like(floor)
    update[...] = jnp.zeros_like(update)
    face_out[...] = jnp.zeros_like(face_out)
    sub = lax.broadcasted_iota(jnp.int32, (8, 128), 0)
    lane = lax.broadcasted_iota(jnp.int32, (8, 128), 1)
    bits = [jnp.where((lane & (1 << bit)) != 0, 1.0, 0.0) for bit in range(7)]
    k_mask = jnp.where(sub < 5, 1.0, 0.0)
    for node in range(5):
        column = jnp.zeros((8, 128), jnp.float32)
        for row in range(5):
            if TABLE[row, node] != 0.0:
                column = jnp.where(sub == row, float(TABLE[row, node]), column)
        coef[COL_D + node] = column

    lane1 = lax.broadcasted_iota(jnp.int32, (1, 128), 1)
    high1 = (lane1 & 64) != 0
    low1 = (lane1 & 32) != 0

    def element_row(ref):
        return jnp.where(
            high1,
            jnp.where(low1, ref[1, 0, 1], ref[1, 0, 0]),
            jnp.where(low1, ref[0, 0, 1], ref[0, 0, 0]),
        )

    def column_row(ref):
        return jnp.where(high1, ref[1, 0].astype(jnp.float32), ref[0, 0].astype(jnp.float32))

    load.wait()
    fields = swap_bits([staged[e // 2, 0, e % 2] for e in range(4)], FIELD_BITS)
    for field in range(4):
        nat[field, 0:125] = fields[field]
    nat[0, 125:126] = element_row(bulk)
    nat[0, 126:127] = element_row(buoy)
    nat[0, 127:128] = column_row(layers)
    cell_row = column_row(cells)
    nat[1, 125:126] = cell_row
    nat[1, 126:127] = cell_row
    nat[1, 127:128] = cell_row
    for field in (2, 3):
        nat[field, 125:128] = jnp.zeros((3, 128), jnp.float32)
    blocks = swap_bits([nat[:, 16 * at : 16 * at + 16, :] for at in range(8)], RANK_BITS)
    for at in range(8):
        pack_out[at] = blocks[at]

    pl.semaphore_wait(barrier, len(greeted))

    def swap_copy(out_ref, in_ref, send, recv, delta, by_owner=False):
        device, rank, to_y = partner(delta)
        return pltpu.make_async_remote_copy(
            src_ref=out_ref.at[to_y if by_owner else rank],
            dst_ref=in_ref.at[me],
            send_sem=send.at[delta],
            recv_sem=recv.at[delta],
            device_id=device,
            device_id_type=MESH,
        )

    order = (2, 3, 4, 5, 6, 7, 1)
    sends = [swap_copy(pack_out, pack_in, a_send, a_recv, delta) for delta in order]
    for copy in sends:
        copy.start()
    pack_in[me] = pack_out[me]
    for copy in sends:
        copy.wait_recv()

    blocks = swap_bits([pack_in[at] for at in range(8)], RANK_BITS)
    for at in range(8):
        nat[:, 16 * at : 16 * at + 16, :] = blocks[at]

    def wide(row):
        return jnp.broadcast_to(row, (8, 128))

    bulk_l = wide(nat[0, 125:126])
    buoy_l = wide(nat[0, 126:127])
    layers_l = wide(nat[0, 127:128])
    depth = 4.0 * bits[3] + 2.0 * bits[2] + bits[5]
    active = jnp.where(depth < layers_l, 1.0, 0.0)
    coef[SELECT] = jnp.where(depth == layers_l - 1.0, 1.0, 0.0)
    act_k = active * k_mask
    coef[ACTIVE] = act_k

    for line in range(25):
        state[0, :, 8 * line : 8 * line + 8, :] = nat[:, 5 * line : 5 * line + 8, :] * act_k

    def face_rows(ref, field, axis, side):
        node = 4 * side
        if axis == 0:
            return ref[field, 40 * node : 40 * node + 40, :].reshape(5, 8, 128)
        return jnp.stack([ref[field, 40 * i + 8 * node : 40 * i + 8 * node + 8, :] for i in range(5)])

    def face_copy(section, direction):
        return pltpu.make_async_remote_copy(
            src_ref=face_out.at[section, direction],
            dst_ref=face_in.at[section, direction],
            send_sem=h_send.at[section, direction],
            recv_sem=h_recv.at[section, direction],
            device_id=neighbours[direction + 1 - 2 * (direction % 2)],
            device_id_type=MESH,
        )

    def pack_two(first, second, direction):
        axis, side, bit, shift = face_of(direction)
        mask = bit_mask(first.shape, bit)
        moved = lane_roll(first, shift)
        return jnp.where(mask, moved, second) if side == 1 else jnp.where(mask, second, moved)

    def send_faces(section, ref, first):
        for direction in (2, 3, 0, 1):
            axis, side, bit, shift = face_of(direction)
            others = [1, 2, 3]
            others.remove(1 + axis)
            for half, (one, two) in enumerate(((0, 1 + axis), (others[0], others[1]))):
                packed = pack_two(
                    face_rows(ref, one, axis, 1 - side), face_rows(ref, two, axis, 1 - side), direction
                )
                for line in range(5):
                    at = 25 * half + 5 * line
                    face_out[section, direction, at : at + 8, :] = packed[line]
            if first:
                face_out[section, direction, 48:56, :] = jnp.where(
                    sub >= 5, pack_two(bulk_l, buoy_l, direction),
                    face_out[section, direction, 48:56, :],
                )
            face_copy(section, direction).start()

    send_faces(0, state.at[0], True)

    speed_l = jnp.sqrt(bulk_l * buoy_l)
    coef[BULK] = bulk_l
    coef[BUOY] = buoy_l
    coef[SPEED] = speed_l
    coef[VOL_B] = buoy_l * act_k
    coef[VOL_K] = bulk_l * act_k
    coef[VOL_G] = GRAVITY / buoy_l * act_k
    for direction in range(4):
        axis, side, bit, _ = face_of(direction)
        width = 1 << bit
        shift = width if side == 0 else -width
        mask = bits[bit] if side == 0 else 1.0 - bits[bit]
        use = 5.0 * act_k * mask
        sign = 1.0 if side == 1 else -1.0
        at = INNER + 3 * direction
        coef[at] = use * jnp.maximum(speed_l, lane_roll(speed_l, shift))
        coef[at + 1] = sign * use * lane_roll(buoy_l, shift)
        coef[at + 2] = sign * use * lane_roll(bulk_l, shift)

    def deeper(value, side):
        mask = bit_mask(value.shape, 5)
        if side == 0:
            return jnp.where(mask, lane_roll(value, 32), lane_roll(value, -28))
        return jnp.where(mask, lane_roll(value, 28), lane_roll(value, -32))

    for side in range(2):
        inside = jnp.where(depth > 0.5, 1.0, 0.0) if side == 0 else jnp.where(depth < 6.5, 1.0, 0.0)
        sign = 1.0 if side == 1 else -1.0
        jump = 5.0 * active * jnp.maximum(speed_l, inside * deeper(speed_l, side))
        at = Z_ROWS + 4 * side
        coef[at] = jump
        coef[at + 1] = jump * inside
        coef[at + 2] = sign * 5.0 * active * inside * deeper(buoy_l, side)
        coef[at + 3] = sign * 5.0 * active * inside * deeper(bulk_l, side)

    def row(index):
        return coef[index, 0:1, :]

    def trace_copy(steps):
        return pltpu.make_async_remote_copy(
            src_ref=tr_out,
            dst_ref=tr_in.at[steps - 1],
            send_sem=t_send.at[steps - 1],
            recv_sem=t_recv.at[steps - 1],
            device_id=along(steps),
            device_id_type=MESH,
        )

    def section(number, carry):
        now = lax.rem(number, 2)
        later = 1 - now
        stage = lax.rem(number, 4)
        ends = (stage == 0) | (stage == 3)
        share = jnp.where(ends, DT / 6.0, DT / 3.0).astype(jnp.float32)
        reach = jnp.where(stage == 3, DT / 6.0, jnp.where(stage == 2, DT, DT / 2.0)).astype(jnp.float32)
        keep = jnp.where(stage == 0, 0.0, 1.0).astype(jnp.float32)
        last = jnp.where(stage == 3, 1.0, 0.0).astype(jnp.float32)
        here, there = state.at[now], state.at[later]

        @pl.when(stage == 0)
        def _():
            base[...] = here[...]

        top = [here[field, pl.ds(0, 25, stride=8), :] for field in range(4)]
        bottom = [here[field, pl.ds(4, 25, stride=8), :] for field in range(4)]
        for field in range(4):
            floor[field] += share * bottom[field]

        @pl.when(number == SECTIONS - 1)
        def _():
            chosen = [floor[field] * row(SELECT) for field in range(4)]
            together = fold_bits(chosen, (2, 3))
            together = together + flip(together, 5)
            tr_out[0:25] = together
            tr_out[25:26] = nat[1, 125:126]
            tr_out[26:32] = jnp.zeros((6, 128), jnp.float32)
            from_lane = lax.broadcasted_iota(jnp.int32, (128, 128), 0)
            to_lane = lax.broadcasted_iota(jnp.int32, (128, 128), 1)
            wanted = jnp.zeros((128, 128), jnp.int32)
            for to_bit, from_bit in ((6, 3), (5, 2), (3, 6), (2, 4), (1, 1), (0, 0)):
                wanted = wanted + jnp.where((to_lane & (1 << to_bit)) != 0, 1 << from_bit, 0)
            table = jnp.where((from_lane == wanted) & ((to_lane & 16) == 0), 1.0, 0.0)
            tr_out[...] = jnp.dot(
                tr_out[...], table, precision=lax.Precision.HIGHEST,
                preferred_element_type=jnp.float32,
            )
            for steps in (1, 2):
                trace_copy(steps).start()

        def cube(field):
            return here[field].reshape(5, 5, 8, 128)

        def along_i(value):
            return jnp.stack([weighted(TABLE[i], [value[m] for m in range(5)]) for i in range(5)])

        def along_j(value):
            return jnp.stack(
                [weighted(TABLE[j], [value[:, m] for m in range(5)]) for j in range(5)], axis=1
            )

        def along_k(value):
            total = None
            for node in range(5):
                one = jnp.broadcast_to(value[:, :, node : node + 1, :], (5, 5, 8, 128))
                term = coef[COL_D + node] * one
                total = term if total is None else total + term
            return total

        def put(field, value):
            rate[field] = value.reshape(200, 128)

        pressure = cube(0)
        put(1, coef[VOL_K] * along_i(pressure))
        put(2, coef[VOL_K] * along_j(pressure))
        put(3, coef[VOL_K] * along_k(pressure) + coef[VOL_G] * pressure)
        put(0, coef[VOL_B] * (along_i(cube(1)) + along_j(cube(2)) + along_k(cube(3))))

        for direction in range(4):
            axis, side, bit, _ = face_of(direction)
            width = 1 << bit
            shift = width if side == 0 else -width
            at = INNER + 3 * direction
            outer = [lane_roll(face_rows(here, field, axis, 1 - side), shift) for field in range(4)]
            for field in range(4):
                add = coef[at] * (outer[field] - face_rows(here, field, axis, side))
                if field == 0:
                    add = add + coef[at + 1] * outer[1 + axis]
                if field == 1 + axis:
                    add = add + coef[at + 2] * outer[0]
                add_face(rate, field, axis, side, add, None)
        for side in range(2):
            at = Z_ROWS + 4 * side
            own = bottom if side == 1 else top
            outer = [deeper((top if side == 1 else bottom)[field], side) for field in range(4)]
            for field in range(4):
                add = row(at + 1) * outer[field] - row(at) * own[field]
                if field == 0:
                    add = add + row(at + 2) * outer[3]
                if field == 3:
                    add = add + row(at + 3) * outer[0]
                where = pl.ds(4 * side, 25, stride=8)
                rate[field, where, :] = rate[field, where, :] + add

        for field in range(4):
            now_rate = rate[field]
            before = update[field]
            there[field] = base[field] + (reach * now_rate + last * before)
            update[field] = keep * before + share * now_rate

        for direction in (2, 3, 0, 1):
            face_copy(number, direction).wait_recv()

        @pl.when(number == 0)
        def _():
            for direction in range(4):
                axis, side, bit, shift = face_of(direction)
                packed = jnp.broadcast_to(face_in[0, direction, 53:54, :], (8, 128))
                bulk_o, buoy_o = packed, lane_roll(packed, shift)
                if axis == 0:
                    limit = gx == (N_GX - 1 if side == 1 else 0)
                else:
                    limit = zc == (N_ZC - 1 if side == 1 else 0)
                inside = jnp.where(limit, 0.0, 1.0).astype(jnp.float32)
                mask = bits[bit] if side == 1 else 1.0 - bits[bit]
                use = 5.0 * coef[ACTIVE] * mask
                sign = 1.0 if side == 1 else -1.0
                jump = use * jnp.maximum(coef[SPEED], inside * jnp.sqrt(bulk_o * buoy_o))
                at = OUTER + 4 * direction
                coef[at] = jump
                coef[at + 1] = jump * inside
                coef[at + 2] = sign * inside * use * buoy_o
                coef[at + 3] = sign * inside * use * bulk_o

        for direction in range(4):
            axis, side, bit, shift = face_of(direction)
            others = [1, 2, 3]
            others.remove(1 + axis)
            at = OUTER + 4 * direction
            arrived = []
            for half in range(2):
                packed = jnp.stack(
                    [
                        face_in[number, direction, 25 * half + 5 * line : 25 * half + 5 * line + 8, :]
                        for line in range(5)
                    ]
                )
                arrived += [packed, lane_roll(packed, shift)]
            by_field = {0: arrived[0], 1 + axis: arrived[1], others[0]: arrived[2], others[1]: arrived[3]}
            for field in range(4):
                add = coef[at + 1] * by_field[field] - coef[at] * face_rows(here, field, axis, side)
                if field == 0:
                    add = add + coef[at + 2] * by_field[1 + axis]
                if field == 1 + axis:
                    add = add + coef[at + 3] * by_field[0]
                add_face(there, field, axis, side, add, reach)
                add_face(update, field, axis, side, add, share)

        @pl.when(number < SECTIONS - 1)
        def _():
            send_faces(number + 1, there, False)

        return carry

    def add_face(ref, field, axis, side, add, scale):
        node = 4 * side
        if scale is not None:
            add = scale * add
        if axis == 0:
            rows = slice(40 * node, 40 * node + 40)
            ref[field, rows, :] = ref[field, rows, :] + add.reshape(40, 128)
        else:
            for i in range(5):
                rows = slice(40 * i + 8 * node, 40 * i + 8 * node + 8)
                ref[field, rows, :] = ref[field, rows, :] + add[i]

    lax.fori_loop(0, SECTIONS, section, 0)

    for line in range(25):
        nat[:, 5 * line : 5 * line + 8, :] = state[0, :, 8 * line : 8 * line + 8, :]
    blocks = swap_bits([nat[:, 16 * at : 16 * at + 16, :] for at in range(8)], RANK_BITS)
    for at in range(8):
        back_out[at] = blocks[at]
    backs = [swap_copy(back_out, back_in, b_send, b_recv, delta) for delta in order]
    for copy in backs:
        copy.start()
    back_in[me] = back_out[me]

    for steps in (1, 2):
        trace_copy(steps).wait_recv()
    first_cell = ((gx * N_ZC + zc) * (2 * S_DEV)).astype(jnp.float32)
    sources = [tr_out, tr_in.at[0], tr_in.at[1]]
    values = [source[0:25] for source in sources]
    labels = [source[25:26] - first_cell for source in sources]
    for owner in range(2):
        picked = []
        for cell in range(S_DEV):
            total = None
            for value, label in zip(values, labels):
                hit = jnp.where(label == float(owner * S_DEV + cell), 1.0, 0.0)
                term = hit * value
                total = term if total is None else total + term
            picked.append(total)
        tb_out[owner] = fold_bits(picked, (2, 3, 4))
    ends = [swap_copy(tb_out, tb_in, c_send, c_recv, delta, True) for delta in order]
    for copy in ends:
        copy.start()
    tb_in[me] = tb_out[y_lo]

    for copy in backs:
        copy.wait_recv()
    blocks = swap_bits([back_in[at] for at in range(8)], RANK_BITS)
    for at in range(8):
        nat[:, 16 * at : 16 * at + 16, :] = blocks[at]
    elements = swap_bits([nat[field, 0:125] for field in range(4)], FIELD_BITS)
    for e in range(4):
        staged[e // 2, 0, e % 2] = elements[e]
    store = pltpu.make_async_copy(staged, out_hbm, local_sem.at[1])
    store.start()

    for copy in ends:
        copy.wait_recv()
    blocks = swap_bits([tb_in[at] for at in range(8)], RANK_BITS)
    for at in range(8):
        trace[at] = blocks[at]
    store_trace = pltpu.make_async_copy(trace, trace_hbm, local_sem.at[2])
    store_trace.start()

    for copy in sends + backs + ends:
        copy.wait_send()
    for steps in (1, 2):
        trace_copy(steps).wait_send()

    def drain(number, carry):
        for direction in range(4):
            face_copy(number, direction).wait_send()
        return carry

    lax.fori_loop(0, SECTIONS, drain, 0)
    store.wait()
    store_trace.wait()


def shards(adjoint_state, bulk_modulus, buoyancy, water_layers, surface_cell):
    f32 = jnp.float32
    in_smem = pl.BlockSpec(memory_space=pltpu.SMEM)
    in_any = pl.BlockSpec(memory_space=pl.ANY)
    dma = pltpu.SemaphoreType.DMA
    return pl.pallas_call(
        kernel,
        out_shape=(
            jax.ShapeDtypeStruct(adjoint_state.shape, f32),
            jax.ShapeDtypeStruct((S_DEV, 25, 128), f32),
        ),
        in_specs=[in_any, in_smem, in_smem, in_smem, in_smem],
        out_specs=(in_any, in_any),
        scratch_shapes=[
            pltpu.VMEM(adjoint_state.shape, f32),
            pltpu.VMEM((4, 128, 128), f32),
            pltpu.VMEM((8, 4, 16, 128), f32),
            pltpu.VMEM((8, 4, 16, 128), f32),
            pltpu.VMEM((8, 4, 16, 128), f32),
            pltpu.VMEM((8, 4, 16, 128), f32),
            pltpu.VMEM((2, 4, 200, 128), f32),
            pltpu.VMEM((4, 200, 128), f32),
            pltpu.VMEM((4, 200, 128), f32),
            pltpu.VMEM((4, 200, 128), f32),
            pltpu.VMEM((N_COEF, 8, 128), f32),
            pltpu.VMEM((SECTIONS, 4, 56, 128), f32),
            pltpu.VMEM((SECTIONS, 4, 56, 128), f32),
            pltpu.VMEM((4, 25, 128), f32),
            pltpu.VMEM((32, 128), f32),
            pltpu.VMEM((2, 32, 128), f32),
            pltpu.VMEM((2, 25, 128), f32),
            pltpu.VMEM((8, 25, 128), f32),
            pltpu.VMEM((8, 25, 128), f32),
            dma((3,)),
            dma((8,)),
            dma((8,)),
            dma((SECTIONS, 4)),
            dma((SECTIONS, 4)),
            dma((2,)),
            dma((2,)),
            dma((8,)),
            dma((8,)),
            dma((8,)),
            dma((8,)),
        ],
        compiler_params=pltpu.CompilerParams(
            collective_id=0, has_side_effects=True, vmem_limit_bytes=24 * 1024 * 1024
        ),
        name="adjoint_steps",
    )(adjoint_state, bulk_modulus, buoyancy, water_layers, surface_cell)


def solution(mesh):
    placed = (
        P("gx", "gy", "gz", None, None),
        P("gx", "gy", "gz"),
        P("gx", "gy", "gz"),
        P("gx", "gy"),
        P("gx", "gy"),
    )
    return jax.shard_map(
        shards,
        mesh=mesh,
        in_specs=placed,
        out_specs=(P("gx", "gy", "gz", None, None), P(("gx", "gy"), None, None)),
        check_vma=False,
    )
```

profile of v0, /device:TPU:1, one launch (start us, length us, event | category | flops | bytes accessed | tf_op | source)
XLA Modules:
  0.0 58.5 jit_solution(17197081677832000352)
XLA Ops:
  0.6 0.0 copy-start.2
  0.6 0.7 %copy.8.layers = s32[2,1]{1,0:T(2,128)S(1)} copy(s32[2,1]{0,1:T(1,128)} %param.8) | data formatting | bytes 16 | tf_op args[3]
  1.4 0.0 copy-done.2
  1.4 0.1 copy.9.cells
  1.5 0.0 copy-start
  1.5 0.0 copy-start.1
  1.5 1.0 %copy.7.state_hbm = f32[2,1,2,125,128]{4,3,2,1,0:T(8,128)S(1)} copy(f32[2,1,2,125,128]{4,2,3,1,0:T(2,128)} %param.5) | data formatting | bytes 512000 | tf_op args[0]
  2.5 0.0 copy-done
  2.5 0.0 copy-done.1
  2.5 54.3 %adjoint_steps.1 = (f32[2,1,2,125,128]{4,3,2,1,0:T(8,128)S(1)}, f32[8,25,128]{2,1,0:T(8,128)S(1)}) custom-call(f32[2,1,2,125,128]{4,3,2,1,0:T(8,128)S(1)} %copy.7.state_hbm, f32[2,1,2]{2,1,0:T(1,128)S(1)} %copy-done, f32[2,1,2]{2,1,0:T(1,128)S(1)} %copy-done.1, s32[2,1]{1,0:T(2,128)S(1)} %copy.8.layers, s32[2,1]{1,0:T(2,128)S(1)} %copy.9.cells), custom_call_target="tpu_custom_call" | custom-call | tf_op jit(solution)/shard_map/adjoint_steps/pallas_call | solution.py:567
  56.8 0.9 %copy.10 = f32[2,1,2,125,128]{4,2,3,1,0:T(2,128)} copy(f32[2,1,2,125,128]{4,3,2,1,0:T(8,128)S(1)} %get-tuple-element.2) | data formatting | bytes 512000 | tf_op jit(solution)/shard_map/adjoint_steps/pallas_call | solution.py:567
  57.7 0.7 %copy.11 = f32[8,25,128]{2,0,1:T(8,128)} copy(f32[8,25,128]{2,1,0:T(8,128)S(1)} %get-tuple-element.3) | data formatting | bytes 204800 | tf_op jit(solution)/shard_map/adjoint_steps/pallas_call | solution.py:567
Async XLA Ops:
  0.6 0.8 %copy-start.2 = (s32[2,1]{0,1:T(1,128)S(1)}, s32[2,1]{0,1:T(1,128)}, u32[]{:S(2)}) copy-start(s32[2,1]{0,1:T(1,128)} %param.9) | copy-start | bytes 28
  1.5 1.0 %copy-start = (f32[2,1,2]{2,1,0:T(1,128)S(1)}, f32[2,1,2]{2,1,0:T(1,128)}, u32[]{:S(2)}) copy-start(f32[2,1,2]{2,1,0:T(1,128)} %bulk.1) | copy-start | bytes 52
  1.5 1.0 %copy-start.1 = (f32[2,1,2]{2,1,0:T(1,128)S(1)}, f32[2,1,2]{2,1,0:T(1,128)}, u32[]{:S(2)}) copy-start(f32[2,1,2]{2,1,0:T(1,128)} %buoy.1) | copy-start | bytes 52
where the time goes:
time: 58.6 us; the launch traced here: 58.5 us
  Pallas kernels  54.3 us (93%)
  local copies, waits for them, and re-layouts  3.45 us (6%)
  between operations  0.67 us (1%)
    pallas_call x1, Pallas kernels, shards(): pl.pallas_call(kernel, out_shape=(jax.ShapeDtypeStruct(adjoint_state.shap...  54.3 us
    unnamed x9, local copies, waits for them, and re-layouts  1.84 us
    pallas_call x2, local copies, waits for them, and re-layouts, shards(): pl.pallas_call(kernel, out_shape=(jax.ShapeDtypeStruct(adjoint_state.shap...  1.6 us

commit v1 on v0

v1 whole, which is shorter than its diff:
```python
import math

import jax
import jax.numpy as jnp
import numpy as np
from jax import lax
from jax.experimental import pallas as pl
from jax.experimental.pallas import tpu as pltpu
from jax.sharding import PartitionSpec as P

N_ZC = 8
RANKS = 32
STEPS = 2
S_DEV = 8
GRAVITY = 2.0
DT = 0.02
MESH = pl.DeviceIdType.MESH


def derivative_rows():
    points = np.array([-1.0, -math.sqrt(3.0 / 7.0), 0.0, math.sqrt(3.0 / 7.0), 1.0])
    scales = np.array(
        [np.prod([points[a] - points[b] for b in range(5) if b != a]) for a in range(5)]
    )
    table = np.zeros((5, 5))
    for a in range(5):
        for b in range(5):
            if a != b:
                table[a, b] = scales[a] / scales[b] / (points[a] - points[b])
        table[a, a] = -np.sum(table[a])
    table[0, 0] += 5.0
    table[4, 4] -= 5.0
    table[np.abs(table) < 1e-12] = 0.0
    return table


TABLE = derivative_rows()
KAPPA = float(np.dot(TABLE[0], TABLE[:, 0]))


def weighted(row, parts):
    total = None
    for weight, part in zip(row, parts):
        if weight != 0.0:
            term = float(weight) * part
            total = term if total is None else total + term
    return total


def bit_mask(shape, bit):
    lanes = lax.broadcasted_iota(jnp.int32, shape, len(shape) - 1)
    return (lanes & (1 << bit)) != 0


def lane_roll(value, shift):
    return pltpu.roll(value, shift % 128, axis=value.ndim - 1)


def swap_pair(low, high, bit):
    width = 1 << bit
    mask = bit_mask(low.shape, bit)
    return (
        jnp.where(mask, lane_roll(high, width), low),
        jnp.where(mask, high, lane_roll(low, -width)),
    )


def swap_stage(value, index_bit, lane_bit):
    step = 1 << index_bit
    shape = value.shape
    split = value.reshape((shape[0] // (2 * step), 2, step) + shape[1:])
    part = split[:, 0].shape
    flat = (-1,) + shape[-2:]
    low, high = swap_pair(split[:, 0].reshape(flat), split[:, 1].reshape(flat), lane_bit)
    return jnp.stack([low.reshape(part), high.reshape(part)], axis=1).reshape(shape)


def swap_bits(value, count):
    for bit in range(count):
        value = swap_stage(value, bit, bit)
    return value


def flip(value, bit):
    width = 1 << bit
    mask = bit_mask(value.shape, bit)
    return jnp.where(mask, lane_roll(value, width), lane_roll(value, -width))


def fold_pair(low, high, bit):
    mask = bit_mask(low.shape, bit)
    return jnp.where(mask, high, low) + flip(jnp.where(mask, low, high), bit)


def neighbour_lanes(value, axis, side):
    if axis == 1:
        return lane_roll(value, 1 if side == 0 else -1)
    wide, short, bit = (64, 56, 6) if axis == 0 else (32, 30, 5)
    mask = bit_mask(value.shape, bit)
    if side == 0:
        return jnp.where(mask, lane_roll(value, wide), lane_roll(value, -short))
    return jnp.where(mask, lane_roll(value, short), lane_roll(value, -wide))


VOL = 0
FACES = 3
SET = 19
GHOST = SET
INNER = 2 * SET
OUTER = INNER + 6
INTO = OUTER + 4
COL_D = INTO + 5
SELECT = COL_D + 5
BULK, BUOY, ACTIVE, SPEED = SELECT + 1, SELECT + 2, SELECT + 3, SELECT + 4
N_COEF = SPEED + 1


def kernel(
    state_hbm, bulk, buoy, layers, cells, out_hbm, trace_hbm,
    staged, nat, pack_out, pack_in, back_out, back_in, state, update, rate, coef,
    near, ghost, ghost_rate, face_out, face_in, floor, tr_out, tr_in, tb_out, tb_in, trace,
    local_sem, a_send, a_recv, h_send, h_recv, t_send, t_recv, b_send, b_recv, c_send, c_recv,
):
    gx = lax.axis_index("gx")
    gy = lax.axis_index("gy")
    gz = lax.axis_index("gz")
    zc, y_lo = gy // 2, gy % 2
    me = gx * 8 + gz * 2 + y_lo

    load = pltpu.make_async_copy(state_hbm, staged, local_sem.at[0])
    load.start()

    def device_of(rank):
        return (rank // 8, zc * 2 + rank % 2, (rank // 2) % 4)

    def layer(steps):
        return (gx, (gy + 2 * steps + 2 * N_ZC) % (2 * N_ZC), gz)

    barrier = pltpu.get_barrier_semaphore()

    def greet(delta, carry):
        pl.semaphore_signal(
            barrier, inc=1, device_id=device_of((me + delta) % RANKS), device_id_type=MESH
        )
        return carry

    lax.fori_loop(1, RANKS, greet, 0)
    for steps in (1, -1, 2, -2):
        pl.semaphore_signal(barrier, inc=1, device_id=layer(steps), device_id_type=MESH)

    floor[...] = jnp.zeros_like(floor)
    face_out[...] = jnp.zeros_like(face_out)
    sub = lax.broadcasted_iota(jnp.int32, (8, 128), 0)
    lane = lax.broadcasted_iota(jnp.int32, (8, 128), 1)
    bits = [jnp.where((lane & (1 << bit)) != 0, 1.0, 0.0) for bit in range(7)]
    k_mask = jnp.where(sub < 5, 1.0, 0.0)
    for node in range(5):
        column = jnp.zeros((8, 128), jnp.float32)
        for row_at in range(5):
            if TABLE[row_at, node] != 0.0:
                column = jnp.where(sub == row_at, float(TABLE[row_at, node]), column)
        coef[COL_D + node] = column

    lane1 = lax.broadcasted_iota(jnp.int32, (1, 128), 1)
    high1 = (lane1 & 64) != 0
    low1 = (lane1 & 32) != 0

    def element_row(ref):
        return jnp.where(
            high1,
            jnp.where(low1, ref[1, 0, 1], ref[1, 0, 0]),
            jnp.where(low1, ref[0, 0, 1], ref[0, 0, 0]),
        )

    def column_row(ref):
        return jnp.where(high1, ref[0, 1].astype(jnp.float32), ref[0, 0].astype(jnp.float32))

    def blocks_of(ref):
        return jnp.stack(
            [
                jnp.stack([ref[low, 8 * tile : 8 * tile + 8], ref[2 + low, 8 * tile : 8 * tile + 8]])
                for tile in range(16)
                for low in range(2)
            ]
        )

    def put_blocks(ref, value):
        for at in range(32):
            tile, low = at // 2, at % 2
            for high in range(2):
                ref[2 * high + low, 8 * tile : 8 * tile + 8] = value[at, high]

    def field_swap(parts):
        for step, bit in ((1, 5), (2, 6)):
            for at in range(4):
                if not at & step:
                    parts[at], parts[at + step] = swap_pair(parts[at], parts[at + step], bit)
        return parts

    load.wait()
    fields = field_swap([staged[e // 2, 0, :, e % 2, :] for e in range(4)])
    for field in range(4):
        nat[field, 0:125] = fields[field]
    nat[0, 125:126] = element_row(bulk)
    nat[0, 126:127] = element_row(buoy)
    nat[0, 127:128] = column_row(layers)
    cell_row = column_row(cells)
    nat[1, 125:126] = cell_row
    nat[1, 126:127] = cell_row
    nat[1, 127:128] = cell_row
    for field in (2, 3):
        nat[field, 125:128] = jnp.zeros((3, 128), jnp.float32)
    pack_out[...] = swap_bits(blocks_of(nat), 5).reshape(32, 16, 128)

    pl.semaphore_wait(barrier, RANKS - 1 + 4)

    def swap_copy(out_ref, in_ref, send, recv, delta, by_owner):
        rank = (me + delta) % RANKS
        return pltpu.make_async_remote_copy(
            src_ref=out_ref.at[(rank // 8) * 2 + rank % 2 if by_owner else rank],
            dst_ref=in_ref.at[me],
            send_sem=send.at[delta],
            recv_sem=recv.at[delta],
            device_id=device_of(rank),
            device_id_type=MESH,
        )

    def each(work, out_ref, in_ref, send, recv, by_owner=False):
        def one(delta, carry):
            work(swap_copy(out_ref, in_ref, send, recv, delta, by_owner))
            return carry

        lax.fori_loop(1, RANKS, one, 0)

    def start(copy):
        copy.start()

    def arrive(copy):
        copy.wait_recv()

    def leave(copy):
        copy.wait_send()

    into = (pack_out, pack_in, a_send, a_recv)
    each(start, *into)
    pack_in[me] = pack_out[me]
    each(arrive, *into)
    put_blocks(nat, swap_bits(pack_in[...].reshape(32, 2, 8, 128), 5))

    def wide(row_value):
        return jnp.broadcast_to(row_value, (8, 128))

    bulk_l = wide(nat[0, 125:126])
    buoy_l = wide(nat[0, 126:127])
    layers_l = wide(nat[0, 127:128])
    depth = 4.0 * bits[2] + 2.0 * bits[1] + bits[5]
    strike = 4.0 * bits[4] + 2.0 * bits[3] + bits[6]
    active = jnp.where(depth < layers_l, 1.0, 0.0)
    act_k = active * k_mask

    for line in range(25):
        state[0, :, 8 * line : 8 * line + 8, :] = nat[:, 5 * line : 5 * line + 8, :] * act_k

    def face_rows(ref, field, axis, side):
        node = 4 * side
        if axis == 0:
            return ref[field, 40 * node : 40 * node + 40, :].reshape(5, 8, 128)
        return jnp.stack([ref[field, 40 * i + 8 * node : 40 * i + 8 * node + 8, :] for i in range(5)])

    def face_copy(step, number, direction):
        return pltpu.make_async_remote_copy(
            src_ref=face_out.at[step, number, direction],
            dst_ref=face_in.at[step, number, direction],
            send_sem=h_send.at[step, number, direction],
            recv_sem=h_recv.at[step, number, direction],
            device_id=layer(1 - 2 * direction),
            device_id_type=MESH,
        )

    def pack_two(first, second, direction):
        mask = bit_mask(first.shape, 0)
        if direction == 0:
            return jnp.where(mask, second, lane_roll(first, -1))
        return jnp.where(mask, lane_roll(first, 1), second)

    def near_planes(ref):
        out = []
        for field in range(4):
            low, high = face_rows(ref, field, 1, 0), face_rows(ref, field, 1, 1)
            out.append(jnp.where(bit_mask(low.shape, 0), high, low))
        return out

    def send_planes(step, number, planes):
        for direction in range(2):
            for half, (one, two) in enumerate(((0, 2), (1, 3))):
                packed = pack_two(planes[one], planes[two], direction)
                for line in range(5):
                    at = 25 * half + 5 * line
                    face_out[step, number, direction, at : at + 8, :] = packed[line]
            if number == 0:
                extra = jnp.where(
                    sub == 5,
                    pack_two(coef[BULK], coef[BUOY], direction),
                    pack_two(coef[ACTIVE], coef[ACTIVE], direction),
                )
                face_out[step, number, direction, 48:56, :] = jnp.where(
                    sub >= 5, extra, face_out[step, number, direction, 48:56, :]
                )
            face_copy(step, number, direction).start()

    def unpack_two(below, above):
        mask = bit_mask(below.shape, 0)
        return jnp.where(mask, above, below), flip(jnp.where(mask, below, above), 0)

    def arrived_planes(step, number):
        for direction in range(2):
            face_copy(step, number, direction).wait_recv()
        out = []
        for half in range(2):
            rows = [
                jnp.stack(
                    [
                        face_in[step, number, direction, 25 * half + 5 * line : 25 * half + 5 * line + 8, :]
                        for line in range(5)
                    ]
                )
                for direction in range(2)
            ]
            out.append(unpack_two(rows[0], rows[1]))
        return [out[0][0], out[1][0], out[0][1], out[1][1]]

    coef[BULK] = bulk_l
    coef[BUOY] = buoy_l
    coef[ACTIVE] = active
    send_planes(0, 0, near_planes(state.at[0]))

    def element_coefs(at, bulk_e, buoy_e, active_e):
        speed_e = jnp.sqrt(bulk_e * buoy_e)
        use = active_e * k_mask
        coef[at + VOL] = buoy_e * use
        coef[at + VOL + 1] = bulk_e * use
        coef[at + VOL + 2] = GRAVITY / buoy_e * use
        for number, (axis, place) in enumerate(((0, strike), (2, depth))):
            for side in range(2):
                inside = jnp.where(place > 0.5, 1.0, 0.0) if side == 0 else jnp.where(place < 6.5, 1.0, 0.0)
                sign = 1.0 if side == 1 else -1.0
                scale = 5.0 * (use if axis == 0 else active_e)
                jump = scale * jnp.maximum(speed_e, inside * neighbour_lanes(speed_e, axis, side))
                to = at + FACES + 8 * number + 4 * side
                coef[to] = jump
                coef[to + 1] = jump * inside
                coef[to + 2] = sign * scale * inside * neighbour_lanes(buoy_e, axis, side)
                coef[to + 3] = sign * scale * inside * neighbour_lanes(bulk_e, axis, side)
        return speed_e

    speed_l = element_coefs(0, bulk_l, buoy_l, active)
    coef[SPEED] = speed_l
    coef[SELECT] = jnp.where(depth == layers_l - 1.0, 1.0, 0.0)
    for side in range(2):
        use = 5.0 * act_k * (bits[0] if side == 0 else 1.0 - bits[0])
        sign = 1.0 if side == 1 else -1.0
        at = INNER + 3 * side
        coef[at] = use * jnp.maximum(speed_l, neighbour_lanes(speed_l, 1, side))
        coef[at + 1] = sign * use * neighbour_lanes(buoy_l, 1, side)
        coef[at + 2] = sign * use * neighbour_lanes(bulk_l, 1, side)

    def outer_coefs():
        packed = [
            [jnp.broadcast_to(face_in[0, 0, direction, at : at + 1, :], (8, 128)) for direction in range(2)]
            for at in (53, 54)
        ]
        bulk_o, buoy_o = unpack_two(packed[0][0], packed[0][1])
        active_o = unpack_two(packed[1][0], packed[1][1])[0]
        speed_o = element_coefs(GHOST, bulk_o, buoy_o, active_o)
        has_low = jnp.where(zc == 0, 0.0, 1.0).astype(jnp.float32)
        has_high = jnp.where(zc == N_ZC - 1, 0.0, 1.0).astype(jnp.float32)
        inside = has_low * (1.0 - bits[0]) + has_high * bits[0]
        sign = 2.0 * bits[0] - 1.0
        speed = jnp.maximum(coef[SPEED], inside * speed_o)
        use = 5.0 * coef[ACTIVE] * k_mask
        coef[OUTER] = use * speed
        coef[OUTER + 1] = use * speed * inside
        coef[OUTER + 2] = use * sign * inside * buoy_o
        coef[OUTER + 3] = use * sign * inside * bulk_o
        use_o = 5.0 * active_o * k_mask * inside
        coef[INTO] = use_o * speed
        coef[INTO + 1] = use_o * speed
        coef[INTO + 2] = -sign * use_o * coef[BUOY]
        coef[INTO + 3] = -sign * use_o * coef[BULK]
        coef[INTO + 4] = KAPPA * bulk_o * buoy_o * active_o * k_mask

    def row(index):
        return coef[index, 0:1, :]

    def rates(src, dst, planes, base):
        def cube(field):
            return src[field].reshape(5, planes, 8, 128)

        def along_i(value):
            return jnp.stack([weighted(TABLE[i], [value[m] for m in range(5)]) for i in range(5)])

        def along_j(value):
            return jnp.stack(
                [weighted(TABLE[j], [value[:, m] for m in range(5)]) for j in range(5)], axis=1
            )

        def along_k(value):
            total = None
            for node in range(5):
                one = jnp.broadcast_to(value[:, :, node : node + 1, :], value.shape)
                term = coef[COL_D + node] * one
                total = term if total is None else total + term
            return total

        def put(field, value):
            dst[field] = value.reshape(40 * planes, 128)

        vol_b, vol_k, vol_g = coef[base + VOL], coef[base + VOL + 1], coef[base + VOL + 2]
        pressure = cube(0)
        put(1, vol_k * along_i(pressure))
        put(2, vol_k * along_j(pressure) if planes == 5 else jnp.zeros_like(pressure))
        put(3, vol_k * along_k(pressure) + vol_g * pressure)
        total = along_i(cube(1)) + along_k(cube(3))
        if planes == 5:
            total = total + along_j(cube(2))
        put(0, vol_b * total)

        size = 8 * planes

        def x_face(ref, field, side):
            return ref[field, 4 * size * side : 4 * size * side + size, :].reshape(planes, 8, 128)

        for side in range(2):
            at = base + FACES + 4 * side
            outer = [neighbour_lanes(x_face(src, field, 1 - side), 0, side) for field in range(4)]
            for field in range(4):
                add = coef[at + 1] * outer[field] - coef[at] * x_face(src, field, side)
                if field == 0:
                    add = add + coef[at + 2] * outer[1]
                if field == 1:
                    add = add + coef[at + 3] * outer[0]
                rows = slice(4 * size * side, 4 * size * side + size)
                dst[field, rows, :] = dst[field, rows, :] + add.reshape(size, 128)

        if planes == 5:
            for side in range(2):
                at = INNER + 3 * side
                outer = [neighbour_lanes(face_rows(src, field, 1, 1 - side), 1, side) for field in range(4)]
                for field in range(4):
                    add = coef[at] * (outer[field] - face_rows(src, field, 1, side))
                    if field == 0:
                        add = add + coef[at + 1] * outer[2]
                    if field == 2:
                        add = add + coef[at + 2] * outer[0]
                    for i in range(5):
                        rows = slice(40 * i + 32 * side, 40 * i + 32 * side + 8)
                        dst[field, rows, :] = dst[field, rows, :] + add[i]

        lines = [[src[field, pl.ds(4 * side, 5 * planes, stride=8), :] for field in range(4)] for side in range(2)]
        for side in range(2):
            at = base + FACES + 8 + 4 * side
            outer = [neighbour_lanes(lines[1 - side][field], 2, side) for field in range(4)]
            for field in range(4):
                add = row(at + 1) * outer[field] - row(at) * lines[side][field]
                if field == 0:
                    add = add + row(at + 2) * outer[3]
                if field == 3:
                    add = add + row(at + 3) * outer[0]
                where = pl.ds(4 * side, 5 * planes, stride=8)
                dst[field, where, :] = dst[field, where, :] + add

    def flux(at, other, own):
        out = [coef[at + 1] * other[field] - coef[at] * own[field] for field in range(4)]
        out[0] = out[0] + coef[at + 2] * other[2]
        out[2] = out[2] + coef[at + 3] * other[0]
        return out

    def add_outer(ref, adds, scale):
        for field in range(4):
            add = scale * adds[field]
            mask = bit_mask(add.shape, 0)
            low, high = jnp.where(mask, 0.0, add), jnp.where(mask, add, 0.0)
            for i in range(5):
                for part, at in ((low, 40 * i), (high, 40 * i + 32)):
                    ref[field, at : at + 8, :] = ref[field, at : at + 8, :] + part[i]

    def add_floor(ref, share):
        for field in range(4):
            floor[field] += share * ref[field, pl.ds(4, 25, stride=8), :]

    def trace_copy(steps):
        return pltpu.make_async_remote_copy(
            src_ref=tr_out,
            dst_ref=tr_in.at[steps - 1],
            send_sem=t_send.at[steps - 1],
            recv_sem=t_recv.at[steps - 1],
            device_id=layer(steps),
            device_id_type=MESH,
        )

    def send_floor():
        chosen = [floor[field] * row(SELECT) for field in range(4)]
        pair = [fold_pair(chosen[0], chosen[1], 1), fold_pair(chosen[2], chosen[3], 1)]
        together = fold_pair(pair[0], pair[1], 2)
        tr_out[0:25] = together + flip(together, 5)
        tr_out[25:26] = nat[1, 125:126]
        tr_out[26:32] = jnp.zeros((6, 128), jnp.float32)
        for steps in (1, 2):
            trace_copy(steps).start()

    def as_planes(ref):
        return [ref[field].reshape(5, 8, 128) for field in range(4)]

    def put_planes(ref, planes):
        for field in range(4):
            ref[field] = planes[field].reshape(40, 128)

    half, sixth, third = DT / 2.0, DT / 6.0, DT / 3.0
    now, first, second, third_in = state.at[0], state.at[1], state.at[2], state.at[3]

    def time_step(step, carry):
        add_floor(now, sixth)
        rates(now, rate, 5, 0)
        for field in range(4):
            first[field] = now[field] + half * rate[field]
            update[field] = sixth * rate[field]
        send_planes(step, 1, near_planes(first))
        rates(first, rate, 5, 0)
        for field in range(4):
            second[field] = now[field] + half * rate[field]
        planes = near_planes(second)
        send_planes(step, 2, planes)
        put_planes(near, planes)
        rates(near, ghost_rate, 1, 0)

        def across(field):
            value = second[field].reshape(5, 5, 8, 128)
            parts = [value[:, m] for m in range(5)]
            low, high = weighted(TABLE[0], parts), weighted(TABLE[4], parts)
            return jnp.where(bit_mask(low.shape, 0), high, low)

        slopes = as_planes(ghost_rate)
        slopes[0] = slopes[0] + coef[VOL] * across(2)
        slopes[2] = slopes[2] + coef[VOL + 1] * across(0)
        starts = near_planes(now)
        send_planes(step, 3, [starts[field] + DT * slopes[field] for field in range(4)])

        outer = arrived_planes(step, 0)

        @pl.when(step == 0)
        def _():
            outer_coefs()

        own = near_planes(now)
        adds = flux(OUTER, outer, own)
        add_outer(first, adds, half)
        add_outer(update, adds, sixth)
        answer = [half * term for term in flux(INTO, own, outer)]
        put_planes(ghost.at[0], answer)
        free = arrived_planes(step, 1)
        outer = [free[field] + answer[field] for field in range(4)]

        add_floor(first, third)
        rates(first, rate, 5, 0)
        own = near_planes(first)
        adds = flux(OUTER, outer, own)
        for field in range(4):
            second[field] = now[field] + half * rate[field]
            update[field] = update[field] + third * rate[field]
        add_outer(second, adds, half)
        add_outer(update, adds, third)
        rates(ghost.at[0], ghost_rate, 1, GHOST)
        slopes = as_planes(ghost_rate)
        answer = [half * (slopes[field] + term) for field, term in enumerate(flux(INTO, own, outer))]
        put_planes(ghost.at[1], answer)
        free = arrived_planes(step, 2)
        outer = [free[field] + answer[field] for field in range(4)]

        add_floor(second, third)
        rates(second, rate, 5, 0)
        own = near_planes(second)
        adds = flux(OUTER, outer, own)
        for field in range(4):
            third_in[field] = now[field] + DT * rate[field]
            update[field] = update[field] + third * rate[field]
        add_outer(third_in, adds, DT)
        add_outer(update, adds, third)
        rates(ghost.at[1], ghost_rate, 1, GHOST)
        slopes = as_planes(ghost_rate)
        early = as_planes(ghost.at[0])
        for field in (0, 2):
            slopes[field] = slopes[field] + half * (coef[INTO + 4] * early[field])
        answer = [DT * (slopes[field] + term) for field, term in enumerate(flux(INTO, own, outer))]
        free = arrived_planes(step, 3)
        outer = [free[field] + answer[field] for field in range(4)]

        add_floor(third_in, sixth)

        @pl.when(step == STEPS - 1)
        def _():
            send_floor()

        rates(third_in, rate, 5, 0)
        adds = flux(OUTER, outer, near_planes(third_in))
        for field in range(4):
            now[field] = now[field] + update[field] + sixth * rate[field]
        add_outer(now, adds, sixth)

        @pl.when(step < STEPS - 1)
        def _():
            send_planes(step + 1, 0, near_planes(now))

        return carry

    lax.fori_loop(0, STEPS, time_step, 0)

    for line in range(25):
        nat[:, 5 * line : 5 * line + 8, :] = now[:, 8 * line : 8 * line + 8, :]
    back_out[...] = swap_bits(blocks_of(nat), 5).reshape(32, 16, 128)
    back = (back_out, back_in, b_send, b_recv)
    each(start, *back)
    back_in[me] = back_out[me]

    for steps in (1, 2):
        trace_copy(steps).wait_recv()
    from_lane = lax.broadcasted_iota(jnp.int32, (128, 128), 0)
    to_lane = lax.broadcasted_iota(jnp.int32, (128, 128), 1)
    same_field = ((from_lane // 2) % 4 == to_lane // 32) & ((from_lane // 32) % 2 == 0)
    sources = [tr_out, tr_in.at[0], tr_in.at[1]]
    labels = [
        jnp.transpose(jnp.broadcast_to(source[25:26], (128, 128))).astype(jnp.int32) for source in sources
    ]
    for upper in range(2):
        owner = (upper * 2 + (to_lane // 2) % 2) * (2 * N_ZC) + 2 * zc + to_lane % 2
        cell = owner * S_DEV + (to_lane // 4) % 8
        total = None
        for source, label in zip(sources, labels):
            chosen = jnp.where(same_field & (label == cell), 1.0, 0.0)
            term = jnp.dot(
                source[...], chosen, precision=lax.Precision.HIGHEST, preferred_element_type=jnp.float32
            )
            total = term if total is None else total + term
        tb_out[4 * upper : 4 * upper + 4] = swap_bits(total.reshape(4, 8, 128), 2)
    ends = (tb_out, tb_in, c_send, c_recv, True)
    each(start, *ends)
    tb_in[me] = tb_out[gx * 2 + y_lo]

    each(arrive, *back)
    put_blocks(nat, swap_bits(back_in[...].reshape(32, 2, 8, 128), 5))
    elements = field_swap([nat[field, 0:125] for field in range(4)])
    for e in range(4):
        staged[e // 2, 0, :, e % 2, :] = elements[e]
    store = pltpu.make_async_copy(staged, out_hbm, local_sem.at[1])
    store.start()

    each(arrive, *ends)
    sums = swap_bits(tb_in[...], 5).reshape(8, 32, 128)
    for cell in range(S_DEV):
        trace[pl.ds(cell, 25, stride=8), :] = sums[cell, 0:25]
    store_trace = pltpu.make_async_copy(trace, trace_hbm, local_sem.at[2])
    store_trace.start()

    each(leave, *into)
    each(leave, *back)
    each(leave, *ends)
    for steps in (1, 2):
        trace_copy(steps).wait_send()

    def drain(step, carry):
        for number in range(4):
            for direction in range(2):
                face_copy(step, number, direction).wait_send()
        return carry

    lax.fori_loop(0, STEPS, drain, 0)
    store.wait()
    store_trace.wait()


def shards(adjoint_state, bulk_modulus, buoyancy, water_layers, surface_cell):
    f32 = jnp.float32
    in_smem = pl.BlockSpec(memory_space=pltpu.SMEM)
    in_any = pl.BlockSpec(memory_space=pl.ANY)
    dma = pltpu.SemaphoreType.DMA
    by_node = jnp.transpose(adjoint_state, (0, 1, 3, 2, 4))
    out, trace = pl.pallas_call(
        kernel,
        out_shape=(
            jax.ShapeDtypeStruct(by_node.shape, f32),
            jax.ShapeDtypeStruct((S_DEV * 25, 128), f32),
        ),
        in_specs=[in_any, in_smem, in_smem, in_smem, in_smem],
        out_specs=(in_any, in_any),
        scratch_shapes=[
            pltpu.VMEM(by_node.shape, f32),
            pltpu.VMEM((4, 128, 128), f32),
            pltpu.VMEM((32, 16, 128), f32),
            pltpu.VMEM((32, 16, 128), f32),
            pltpu.VMEM((32, 16, 128), f32),
            pltpu.VMEM((32, 16, 128), f32),
            pltpu.VMEM((4, 4, 200, 128), f32),
            pltpu.VMEM((4, 200, 128), f32),
            pltpu.VMEM((4, 200, 128), f32),
            pltpu.VMEM((N_COEF, 8, 128), f32),
            pltpu.VMEM((4, 40, 128), f32),
            pltpu.VMEM((2, 4, 40, 128), f32),
            pltpu.VMEM((4, 40, 128), f32),
            pltpu.VMEM((STEPS, 4, 2, 56, 128), f32),
            pltpu.VMEM((STEPS, 4, 2, 56, 128), f32),
            pltpu.VMEM((4, 25, 128), f32),
            pltpu.VMEM((32, 128), f32),
            pltpu.VMEM((2, 32, 128), f32),
            pltpu.VMEM((8, 8, 128), f32),
            pltpu.VMEM((32, 8, 128), f32),
            pltpu.VMEM((S_DEV * 25, 128), f32),
            dma((3,)),
            dma((RANKS,)),
            dma((RANKS,)),
            dma((STEPS, 4, 2)),
            dma((STEPS, 4, 2)),
            dma((2,)),
            dma((2,)),
            dma((RANKS,)),
            dma((RANKS,)),
            dma((RANKS,)),
            dma((RANKS,)),
        ],
        compiler_params=pltpu.CompilerParams(
            collective_id=0, has_side_effects=True, vmem_limit_bytes=24 * 1024 * 1024
        ),
        name="adjoint_steps",
    )(by_node, bulk_modulus, buoyancy, water_layers.T, surface_cell.T)
    return (
        jnp.transpose(out, (0, 1, 3, 2, 4)),
        jnp.transpose(trace.reshape(25, S_DEV, 128), (1, 0, 2)),
    )


def solution(mesh):
    placed = (
        P("gx", "gy", "gz", None, None),
        P("gx", "gy", "gz"),
        P("gx", "gy", "gz"),
        P("gx", "gy"),
        P("gx", "gy"),
    )
    return jax.shard_map(
        shards,
        mesh=mesh,
        in_specs=placed,
        out_specs=(P("gx", "gy", "gz", None, None), P(("gx", "gy"), None, None)),
        check_vma=False,
    )
```

time: 58.6 us -> 47.4 us (0.81)
  Pallas kernels: 54.3 us -> 43.6 us
    pallas_call x1, Pallas kernels: 54.3 us -> 43.6 us  [shards(): pl.pallas_call(kernel, out_shape=(jax.ShapeDtypeStruct(by_node.shape, f32...]
    pallas_call x2 -> x0, local copies, waits for them, and re-layouts: 1.6 us -> none  [shards(): pl.pallas_call(kernel, out_shape=(jax.ShapeDtypeStruct(adjoint_state.shap...]
    unnamed x9 -> x12, local copies, waits for them, and re-layouts: 1.84 us -> 2.97 us
where the time goes in v1:
time: 47.4 us; the launch traced here: 47.3 us
  Pallas kernels  43.6 us (92%)
  local copies, waits for them, and re-layouts  2.97 us (6%)
  between operations  0.67 us (1%)
    pallas_call x1, Pallas kernels, shards(): pl.pallas_call(kernel, out_shape=(jax.ShapeDtypeStruct(by_node.shape, f32...  43.6 us
    unnamed x12, local copies, waits for them, and re-layouts  2.97 us

profile of v1, /device:TPU:1, one launch (start us, length us, event | category | flops | bytes accessed | tf_op | source)
XLA Modules:
  0.0 47.3 jit_solution(7229165934373111803)
XLA Ops:
  0.6 0.0 copy-start.2
  0.6 0.0 copy-start.4
  0.7 0.0 copy-start.1
  0.7 0.0 copy-start.3
  0.7 0.6 %copy-done.2 = f32[2,1,2]{2,1,0:T(1,128)S(1)} copy-done((f32[2,1,2]{2,1,0:T(1,128)S(1)}, f32[2,1,2]{2,1,0:T(1,128)}, u32[]{:S(2)}) %copy-start.2) | copy-done | bytes 40
  1.3 0.0 copy-done.4
  1.3 0.0 copy-done.1
  1.3 0.0 copy-done.3
  1.3 0.0 copy-start
  1.3 0.9 %copy-done = f32[2,1,2,125,128]{4,2,3,1,0:T(2,128)S(1)} copy-done((f32[2,1,2,125,128]{4,2,3,1,0:T(2,128)S(1)}, f32[2,1,2,125,128]{4,2,3,1,0:T(2,128)}, u32[]{:S(2)}) %copy-start) | copy-done | bytes 256024
  2.3 43.6 %adjoint_steps.1 = (f32[2,1,125,2,128]{4,3,2,1,0:T(2,128)S(1)}, f32[200,128]{1,0:T(8,128)S(1)}) custom-call(f32[2,1,125,2,128]{4,3,2,1,0:T(2,128)S(1)} %bitcast.7, f32[2,1,2]{2,1,0:T(1,128)S(1)} %copy-done.1, f32[2,1,2]{2,1,0:T(1,128)S(1)} %copy-done.2, s32[1,2]{1,0:T(1,128)S(1)} %bitcast.10, s32[1,2]{1,0:T(1,128)S(1)} %bitcast.11), custom_call_target="tpu_custom_call" | custom-call | tf_op jit(solution)/shard_map/adjoint_steps/pallas_call | solution.py:686
  45.9 0.7 %copy.9 = f32[2,1,2,125,128]{4,2,3,1,0:T(2,128)} copy(f32[2,1,2,125,128]{4,2,3,1,0:T(2,128)S(1)} %bitcast.8) | data formatting | bytes 512000
  46.6 0.6 %copy.10 = f32[8,25,128]{2,0,1:T(8,128)} copy(f32[8,25,128]{2,0,1:T(8,128)S(1)} %bitcast.9) | data formatting | bytes 204800
Async XLA Ops:
  0.6 0.7 %copy-start.2 = (f32[2,1,2]{2,1,0:T(1,128)S(1)}, f32[2,1,2]{2,1,0:T(1,128)}, u32[]{:S(2)}) copy-start(f32[2,1,2]{2,1,0:T(1,128)} %buoy.1) | copy-start | bytes 52
  0.6 0.7 %copy-start.4 = (s32[2,1]{0,1:T(1,128)S(1)}, s32[2,1]{0,1:T(1,128)}, u32[]{:S(2)}) copy-start(s32[2,1]{0,1:T(1,128)} %param.9) | copy-start | bytes 28
  0.7 0.7 %copy-start.1 = (f32[2,1,2]{2,1,0:T(1,128)S(1)}, f32[2,1,2]{2,1,0:T(1,128)}, u32[]{:S(2)}) copy-start(f32[2,1,2]{2,1,0:T(1,128)} %bulk.1) | copy-start | bytes 52
  0.7 0.7 %copy-start.3 = (s32[2,1]{0,1:T(1,128)S(1)}, s32[2,1]{0,1:T(1,128)}, u32[]{:S(2)}) copy-start(s32[2,1]{0,1:T(1,128)} %param.8) | copy-start | bytes 28
  1.3 0.9 %copy-start = (f32[2,1,2,125,128]{4,2,3,1,0:T(2,128)S(1)}, f32[2,1,2,125,128]{4,2,3,1,0:T(2,128)}, u32[]{:S(2)}) copy-start(f32[2,1,2,125,128]{4,2,3,1,0:T(2,128)} %param.5) | copy-start | bytes 768004

commit v2 on v1

--- a/solution.py
+++ b/solution.py
@@ -116,9 +116,10 @@
 
 
 def kernel(
-    state_hbm, bulk, buoy, layers, cells, out_hbm, trace_hbm,
+    state_hbm, bulk_hbm, buoy_hbm, layers_hbm, cells_hbm, out, trace,
+    bulk, buoy, layers, cells,
     staged, nat, pack_out, pack_in, back_out, back_in, state, update, rate, coef,
-    near, ghost, ghost_rate, face_out, face_in, floor, tr_out, tr_in, tb_out, tb_in, trace,
+    near, ghost, ghost_rate, face_out, face_in, floor, tr_out, tr_in, label_out, label_in, chosen, tb_out, tb_in,
     local_sem, a_send, a_recv, h_send, h_recv, t_send, t_recv, b_send, b_recv, c_send, c_recv,
 ):
     gx = lax.axis_index("gx")
@@ -129,6 +130,14 @@
 
     load = pltpu.make_async_copy(state_hbm, staged, local_sem.at[0])
     load.start()
+    small = [
+        pltpu.make_async_copy(source, target, local_sem.at[1 + at])
+        for at, (source, target) in enumerate(
+            ((bulk_hbm, bulk), (buoy_hbm, buoy), (layers_hbm, layers), (cells_hbm, cells))
+        )
+    ]
+    for copy in small:
+        copy.start()
 
     def device_of(rank):
         return (rank // 8, zc * 2 + rank % 2, (rank // 2) % 4)
@@ -138,18 +147,50 @@
 
     barrier = pltpu.get_barrier_semaphore()
 
-    def greet(delta, carry):
-        pl.semaphore_signal(
-            barrier, inc=1, device_id=device_of((me + delta) % RANKS), device_id_type=MESH
-        )
-        return carry
-
-    lax.fori_loop(1, RANKS, greet, 0)
-    for steps in (1, -1, 2, -2):
-        pl.semaphore_signal(barrier, inc=1, device_id=layer(steps), device_id_type=MESH)
+    has_below, has_above = zc > 0, zc < N_ZC - 1
+
+    def greet(device):
+        pl.semaphore_signal(barrier, inc=1, device_id=device, device_id_type=MESH)
+
+    for delta in range(1, RANKS):
+        greet(device_of((me + delta) % RANKS))
+
+    @pl.when(has_below)
+    def _():
+        greet(layer(-1))
+
+    @pl.when(has_above)
+    def _():
+        greet(layer(1))
+
+    @pl.when(zc == 0)
+    def _():
+        greet(layer(-1))
+        greet(layer(-2))
+
+    @pl.when(zc == 1)
+    def _():
+        greet(layer(-2))
+
+    greetings = (
+        RANKS - 1
+        + has_below.astype(jnp.int32)
+        + has_above.astype(jnp.int32)
+        + (zc == N_ZC - 2).astype(jnp.int32)
+        + 2 * (zc == N_ZC - 1).astype(jnp.int32)
+    )
 
     floor[...] = jnp.zeros_like(floor)
     face_out[...] = jnp.zeros_like(face_out)
+
+    @pl.when(zc == 0)
+    def _():
+        face_in[:, 0] = jnp.zeros((STEPS, 4, 56, 128), jnp.float32)
+
+    @pl.when(zc == N_ZC - 1)
+    def _():
+        face_in[:, 1] = jnp.zeros((STEPS, 4, 56, 128), jnp.float32)
+
     sub = lax.broadcasted_iota(jnp.int32, (8, 128), 0)
     lane = lax.broadcasted_iota(jnp.int32, (8, 128), 1)
     bits = [jnp.where((lane & (1 << bit)) != 0, 1.0, 0.0) for bit in range(7)]
@@ -198,6 +239,8 @@
         return parts
 
     load.wait()
+    for copy in small:
+        copy.wait()
     fields = field_swap([staged[e // 2, 0, :, e % 2, :] for e in range(4)])
     for field in range(4):
         nat[field, 0:125] = fields[field]
@@ -212,39 +255,41 @@
         nat[field, 125:128] = jnp.zeros((3, 128), jnp.float32)
     pack_out[...] = swap_bits(blocks_of(nat), 5).reshape(32, 16, 128)
 
-    pl.semaphore_wait(barrier, RANKS - 1 + 4)
-
-    def swap_copy(out_ref, in_ref, send, recv, delta, by_owner):
-        rank = (me + delta) % RANKS
+    pl.semaphore_wait(barrier, greetings)
+
+    def start(copy):
+        copy.start()
+
+    def leave(copy):
+        copy.wait_send()
+
+    def swap_start(out_ref, in_ref, send, recv, by_owner=False):
+        for delta in range(1, RANKS):
+            rank = (me + delta) % RANKS
+            pltpu.make_async_remote_copy(
+                src_ref=out_ref.at[(rank // 8) * 2 + rank % 2 if by_owner else rank],
+                dst_ref=in_ref.at[me],
+                send_sem=send,
+                recv_sem=recv,
+                device_id=device_of(rank),
+                device_id_type=MESH,
+            ).start()
+
+    def swap_whole(out_ref, in_ref, send, recv, by_owner=False):
+        others = in_ref.at[pl.ds(0, RANKS - 1)]
         return pltpu.make_async_remote_copy(
-            src_ref=out_ref.at[(rank // 8) * 2 + rank % 2 if by_owner else rank],
-            dst_ref=in_ref.at[me],
-            send_sem=send.at[delta],
-            recv_sem=recv.at[delta],
-            device_id=device_of(rank),
+            src_ref=others,
+            dst_ref=others,
+            send_sem=send,
+            recv_sem=recv,
+            device_id=device_of((me + 1) % RANKS),
             device_id_type=MESH,
         )
 
-    def each(work, out_ref, in_ref, send, recv, by_owner=False):
-        def one(delta, carry):
-            work(swap_copy(out_ref, in_ref, send, recv, delta, by_owner))
-            return carry
-
-        lax.fori_loop(1, RANKS, one, 0)
-
-    def start(copy):
-        copy.start()
-
-    def arrive(copy):
-        copy.wait_recv()
-
-    def leave(copy):
-        copy.wait_send()
-
     into = (pack_out, pack_in, a_send, a_recv)
-    each(start, *into)
+    swap_start(*into)
     pack_in[me] = pack_out[me]
-    each(arrive, *into)
+    swap_whole(*into).wait_recv()
     put_blocks(nat, swap_bits(pack_in[...].reshape(32, 2, 8, 128), 5))
 
     def wide(row_value):
@@ -269,13 +314,23 @@
 
     def face_copy(step, number, direction):
         return pltpu.make_async_remote_copy(
-            src_ref=face_out.at[step, number, direction],
-            dst_ref=face_in.at[step, number, direction],
-            send_sem=h_send.at[step, number, direction],
-            recv_sem=h_recv.at[step, number, direction],
+            src_ref=face_out.at[step, direction, number],
+            dst_ref=face_in.at[step, direction, number],
+            send_sem=h_send.at[step, direction],
+            recv_sem=h_recv.at[step, direction, number],
             device_id=layer(1 - 2 * direction),
             device_id_type=MESH,
         )
+
+    def face_do(step, number, direction, work):
+        @pl.when(has_above if direction == 0 else has_below)
+        def _():
+            work(face_copy(step, number, direction))
+
+    def face_wait(step, number, direction):
+        @pl.when(has_below if direction == 0 else has_above)
+        def _():
+            face_copy(step, number, direction).wait_recv()
 
     def pack_two(first, second, direction):
         mask = bit_mask(first.shape, 0)
@@ -296,17 +351,17 @@
                 packed = pack_two(planes[one], planes[two], direction)
                 for line in range(5):
                     at = 25 * half + 5 * line
-                    face_out[step, number, direction, at : at + 8, :] = packed[line]
+                    face_out[step, direction, number, at : at + 8, :] = packed[line]
             if number == 0:
                 extra = jnp.where(
                     sub == 5,
                     pack_two(coef[BULK], coef[BUOY], direction),
                     pack_two(coef[ACTIVE], coef[ACTIVE], direction),
                 )
-                face_out[step, number, direction, 48:56, :] = jnp.where(
-                    sub >= 5, extra, face_out[step, number, direction, 48:56, :]
+                face_out[step, direction, number, 48:56, :] = jnp.where(
+                    sub >= 5, extra, face_out[step, direction, number, 48:56, :]
                 )
-            face_copy(step, number, direction).start()
+            face_do(step, number, direction, start)
 
     def unpack_two(below, above):
         mask = bit_mask(below.shape, 0)
@@ -314,13 +369,13 @@
 
     def arrived_planes(step, number):
         for direction in range(2):
-            face_copy(step, number, direction).wait_recv()
+            face_wait(step, number, direction)
         out = []
         for half in range(2):
             rows = [
                 jnp.stack(
                     [
-                        face_in[step, number, direction, 25 * half + 5 * line : 25 * half + 5 * line + 8, :]
+                        face_in[step, direction, number, 25 * half + 5 * line : 25 * half + 5 * line + 8, :]
                         for line in range(5)
                     ]
                 )
@@ -366,15 +421,16 @@
 
     def outer_coefs():
         packed = [
-            [jnp.broadcast_to(face_in[0, 0, direction, at : at + 1, :], (8, 128)) for direction in range(2)]
+            [jnp.broadcast_to(face_in[0, direction, 0, at : at + 1, :], (8, 128)) for direction in range(2)]
             for at in (53, 54)
         ]
         bulk_o, buoy_o = unpack_two(packed[0][0], packed[0][1])
         active_o = unpack_two(packed[1][0], packed[1][1])[0]
-        speed_o = element_coefs(GHOST, bulk_o, buoy_o, active_o)
         has_low = jnp.where(zc == 0, 0.0, 1.0).astype(jnp.float32)
         has_high = jnp.where(zc == N_ZC - 1, 0.0, 1.0).astype(jnp.float32)
         inside = has_low * (1.0 - bits[0]) + has_high * bits[0]
+        buoy_o = buoy_o + (1.0 - inside)
+        speed_o = element_coefs(GHOST, bulk_o, buoy_o, active_o)
         sign = 2.0 * bits[0] - 1.0
         speed = jnp.maximum(coef[SPEED], inside * speed_o)
         use = 5.0 * coef[ACTIVE] * k_mask
@@ -488,12 +544,13 @@
         for field in range(4):
             floor[field] += share * ref[field, pl.ds(4, 25, stride=8), :]
 
-    def trace_copy(steps):
+    def trace_copy(steps, labels=False):
+        part = 2 * (steps - 1) + (1 if labels else 0)
         return pltpu.make_async_remote_copy(
-            src_ref=tr_out,
-            dst_ref=tr_in.at[steps - 1],
-            send_sem=t_send.at[steps - 1],
-            recv_sem=t_recv.at[steps - 1],
+            src_ref=label_out if labels else tr_out,
+            dst_ref=(label_in if labels else tr_in).at[steps - 1],
+            send_sem=t_send.at[part],
+            recv_sem=t_recv.at[part],
             device_id=layer(steps),
             device_id_type=MESH,
         )
@@ -503,8 +560,7 @@
         pair = [fold_pair(chosen[0], chosen[1], 1), fold_pair(chosen[2], chosen[3], 1)]
         together = fold_pair(pair[0], pair[1], 2)
         tr_out[0:25] = together + flip(together, 5)
-        tr_out[25:26] = nat[1, 125:126]
-        tr_out[26:32] = jnp.zeros((6, 128), jnp.float32)
+        tr_out[25:32] = jnp.zeros((7, 128), jnp.float32)
         for steps in (1, 2):
             trace_copy(steps).start()
 
@@ -528,6 +584,7 @@
         rates(first, rate, 5, 0)
         for field in range(4):
             second[field] = now[field] + half * rate[field]
+            update[field] = update[field] + third * rate[field]
         planes = near_planes(second)
         send_planes(step, 2, planes)
         put_planes(near, planes)
@@ -550,6 +607,9 @@
         @pl.when(step == 0)
         def _():
             outer_coefs()
+            label_out[...] = wide(nat[1, 125:126])
+            for steps in (1, 2):
+                trace_copy(steps, True).start()
 
         own = near_planes(now)
         adds = flux(OUTER, outer, own)
@@ -561,14 +621,23 @@
         outer = [free[field] + answer[field] for field in range(4)]
 
         add_floor(first, third)
-        rates(first, rate, 5, 0)
         own = near_planes(first)
-        adds = flux(OUTER, outer, own)
-        for field in range(4):
-            second[field] = now[field] + half * rate[field]
-            update[field] = update[field] + third * rate[field]
+        came = [half * add for add in adds]
+        put_planes(near, came)
+        rates(near, ghost_rate, 1, 0)
+        slopes = as_planes(ghost_rate)
+        adds = [slopes[field] + term for field, term in enumerate(flux(OUTER, outer, own))]
         add_outer(second, adds, half)
         add_outer(update, adds, third)
+        for field, source, scale in ((0, 2, coef[VOL]), (2, 0, coef[VOL + 1])):
+            inward = scale * came[source]
+            for j in range(5):
+                weight = jnp.where((lane & 1) != 0, float(TABLE[j, 4]), float(TABLE[j, 0]))
+                term = weight * inward
+                for i in range(5):
+                    at = 40 * i + 8 * j
+                    second[field, at : at + 8, :] = second[field, at : at + 8, :] + half * term[i]
+                    update[field, at : at + 8, :] = update[field, at : at + 8, :] + third * term[i]
         rates(ghost.at[0], ghost_rate, 1, GHOST)
         slopes = as_planes(ghost_rate)
         answer = [half * (slopes[field] + term) for field, term in enumerate(flux(INTO, own, outer))]
@@ -618,68 +687,74 @@
         nat[:, 5 * line : 5 * line + 8, :] = now[:, 8 * line : 8 * line + 8, :]
     back_out[...] = swap_bits(blocks_of(nat), 5).reshape(32, 16, 128)
     back = (back_out, back_in, b_send, b_recv)
-    each(start, *back)
+    swap_start(*back)
     back_in[me] = back_out[me]
 
     for steps in (1, 2):
-        trace_copy(steps).wait_recv()
+        trace_copy(steps, True).wait_recv()
     from_lane = lax.broadcasted_iota(jnp.int32, (128, 128), 0)
     to_lane = lax.broadcasted_iota(jnp.int32, (128, 128), 1)
     same_field = ((from_lane // 2) % 4 == to_lane // 32) & ((from_lane // 32) % 2 == 0)
-    sources = [tr_out, tr_in.at[0], tr_in.at[1]]
-    labels = [
-        jnp.transpose(jnp.broadcast_to(source[25:26], (128, 128))).astype(jnp.int32) for source in sources
-    ]
+    for at, source in enumerate((label_out, label_in.at[0], label_in.at[1])):
+        label = jnp.transpose(jnp.broadcast_to(source[0:1], (128, 128))).astype(jnp.int32)
+        for upper in range(2):
+            owner = (upper * 2 + (to_lane // 2) % 2) * (2 * N_ZC) + 2 * zc + to_lane % 2
+            cell = owner * S_DEV + (to_lane // 4) % 8
+            chosen[128 * at : 128 * at + 128, 128 * upper : 128 * upper + 128] = jnp.where(
+                same_field & (label == cell), 1.0, 0.0
+            )
+    for steps in (1, 2):
+        trace_copy(steps).wait_recv()
+    total = jnp.dot(
+        jnp.concatenate([tr_out[...], tr_in[0], tr_in[1]], axis=1), chosen[...],
+        precision=lax.Precision.HIGHEST, preferred_element_type=jnp.float32,
+    )
     for upper in range(2):
-        owner = (upper * 2 + (to_lane // 2) % 2) * (2 * N_ZC) + 2 * zc + to_lane % 2
-        cell = owner * S_DEV + (to_lane // 4) % 8
-        total = None
-        for source, label in zip(sources, labels):
-            chosen = jnp.where(same_field & (label == cell), 1.0, 0.0)
-            term = jnp.dot(
-                source[...], chosen, precision=lax.Precision.HIGHEST, preferred_element_type=jnp.float32
-            )
-            total = term if total is None else total + term
-        tb_out[4 * upper : 4 * upper + 4] = swap_bits(total.reshape(4, 8, 128), 2)
+        part = total[:, 128 * upper : 128 * upper + 128]
+        tb_out[4 * upper : 4 * upper + 4] = swap_bits(part.reshape(4, 8, 128), 2)
     ends = (tb_out, tb_in, c_send, c_recv, True)
-    each(start, *ends)
+    swap_start(*ends)
     tb_in[me] = tb_out[gx * 2 + y_lo]
 
-    each(arrive, *back)
+    swap_whole(*back).wait_recv()
     put_blocks(nat, swap_bits(back_in[...].reshape(32, 2, 8, 128), 5))
     elements = field_swap([nat[field, 0:125] for field in range(4)])
     for e in range(4):
-        staged[e // 2, 0, :, e % 2, :] = elements[e]
-    store = pltpu.make_async_copy(staged, out_hbm, local_sem.at[1])
-    store.start()
-
-    each(arrive, *ends)
+        out[e // 2, 0, :, e % 2, :] = elements[e]
+
+    swap_whole(*ends).wait_recv()
     sums = swap_bits(tb_in[...], 5).reshape(8, 32, 128)
     for cell in range(S_DEV):
         trace[pl.ds(cell, 25, stride=8), :] = sums[cell, 0:25]
-    store_trace = pltpu.make_async_copy(trace, trace_hbm, local_sem.at[2])
-    store_trace.start()
-
-    each(leave, *into)
-    each(leave, *back)
-    each(leave, *ends)
+
+    for swap in (into, back, ends):
+        swap_whole(*swap).wait_send()
     for steps in (1, 2):
         trace_copy(steps).wait_send()
+        trace_copy(steps, True).wait_send()
 
     def drain(step, carry):
-        for number in range(4):
-            for direction in range(2):
-                face_copy(step, number, direction).wait_send()
+        for direction in range(2):
+            sent = face_out.at[step, direction]
+
+            @pl.when(has_above if direction == 0 else has_below)
+            def _():
+                pltpu.make_async_remote_copy(
+                    src_ref=sent,
+                    dst_ref=face_in.at[step, direction],
+                    send_sem=h_send.at[step, direction],
+                    recv_sem=h_recv.at[step, direction, 0],
+                    device_id=layer(1 - 2 * direction),
+                    device_id_type=MESH,
+                ).wait_send()
+
         return carry
 
     lax.fori_loop(0, STEPS, drain, 0)
-    store.wait()
-    store_trace.wait()
 
 
 def shards(adjoint_state, bulk_modulus, buoyancy, water_layers, surface_cell):
     f32 = jnp.float32
-    in_smem = pl.BlockSpec(memory_space=pltpu.SMEM)
     in_any = pl.BlockSpec(memory_space=pl.ANY)
     dma = pltpu.SemaphoreType.DMA
     by_node = jnp.transpose(adjoint_state, (0, 1, 3, 2, 4))
@@ -689,9 +764,13 @@
             jax.ShapeDtypeStruct(by_node.shape, f32),
             jax.ShapeDtypeStruct((S_DEV * 25, 128), f32),
         ),
-        in_specs=[in_any, in_smem, in_smem, in_smem, in_smem],
-        out_specs=(in_any, in_any),
+        in_specs=[in_any] * 5,
+        out_specs=(pl.BlockSpec(memory_space=pltpu.VMEM),) * 2,
         scratch_shapes=[
+            pltpu.SMEM(bulk_modulus.shape, f32),
+            pltpu.SMEM(buoyancy.shape, f32),
+            pltpu.SMEM(water_layers.T.shape, jnp.int32),
+            pltpu.SMEM(surface_cell.T.shape, jnp.int32),
             pltpu.VMEM(by_node.shape, f32),
             pltpu.VMEM((4, 128, 128), f32),
             pltpu.VMEM((32, 16, 128), f32),
@@ -705,28 +784,30 @@
             pltpu.VMEM((4, 40, 128), f32),
             pltpu.VMEM((2, 4, 40, 128), f32),
             pltpu.VMEM((4, 40, 128), f32),
-            pltpu.VMEM((STEPS, 4, 2, 56, 128), f32),
-            pltpu.VMEM((STEPS, 4, 2, 56, 128), f32),
+            pltpu.VMEM((STEPS, 2, 4, 56, 128), f32),
+            pltpu.VMEM((STEPS, 2, 4, 56, 128), f32),
             pltpu.VMEM((4, 25, 128), f32),
             pltpu.VMEM((32, 128), f32),
             pltpu.VMEM((2, 32, 128), f32),
+            pltpu.VMEM((8, 128), f32),
+            pltpu.VMEM((2, 8, 128), f32),
+            pltpu.VMEM((384, 256), f32),
             pltpu.VMEM((8, 8, 128), f32),
             pltpu.VMEM((32, 8, 128), f32),
-            pltpu.VMEM((S_DEV * 25, 128), f32),
-            dma((3,)),
-            dma((RANKS,)),
-            dma((RANKS,)),
-            dma((STEPS, 4, 2)),
-            dma((STEPS, 4, 2)),
-            dma((2,)),
-            dma((2,)),
-            dma((RANKS,)),
-            dma((RANKS,)),
-            dma((RANKS,)),
-            dma((RANKS,)),
+            dma((5,)),
+            dma,
+            dma,
+            dma((STEPS, 2)),
+            dma((STEPS, 2, 4)),
+            dma((4,)),
+            dma((4,)),
+            dma,
+            dma,
+            dma,
+            dma,
         ],
         compiler_params=pltpu.CompilerParams(
-            collective_id=0, has_side_effects=True, vmem_limit_bytes=24 * 1024 * 1024
+            collective_id=0, has_side_effects=True, vmem_limit_bytes=54656 * 1024
         ),
         name="adjoint_steps",
     )(by_node, bulk_modulus, buoyancy, water_layers.T, surface_cell.T)

time: 47.4 us -> 41.9 us (0.88)
  Pallas kernels: 43.6 us -> 39.1 us
  local copies, waits for them, and re-layouts: 2.97 us -> 2.02 us
    pallas_call x1, Pallas kernels: 43.6 us -> 39.1 us  [shards(): pl.pallas_call(kernel, out_shape=(jax.ShapeDtypeStruct(by_node.shape, f32...]
    unnamed x12 -> x10, local copies, waits for them, and re-layouts: 2.97 us -> 2.02 us
where the time goes in v2:
time: 41.9 us; the launch traced here: 41.8 us
  Pallas kernels  39.1 us (93%)
  local copies, waits for them, and re-layouts  2.02 us (5%)
  between operations  0.67 us (2%)
    pallas_call x1, Pallas kernels, shards(): pl.pallas_call(kernel, out_shape=(jax.ShapeDtypeStruct(by_node.shape, f32...  39.1 us
    unnamed x10, local copies, waits for them, and re-layouts  2.02 us

profile of v2, /device:TPU:1, one launch (start us, length us, event | category | flops | bytes accessed | tf_op | source)
XLA Modules:
  0.0 41.8 jit_solution(305632414930225056)
XLA Ops:
  0.6 0.0 copy-start.1
  0.6 0.0 copy-start.3
  0.7 0.0 copy-start
  0.7 0.0 copy-start.2
  0.7 0.6 %copy-done.1 = f32[2,1,2]{2,1,0:T(1,128)S(1)} copy-done((f32[2,1,2]{2,1,0:T(1,128)S(1)}, f32[2,1,2]{2,1,0:T(1,128)}, u32[]{:S(2)}) %copy-start.1) | copy-done | bytes 40
  1.3 0.0 copy-done.3
  1.3 0.0 copy-done
  1.3 0.0 copy-done.2
  1.3 39.1 %adjoint_steps.1 = (f32[2,1,125,2,128]{4,3,2,1,0:T(2,128)S(1)}, f32[200,128]{1,0:T(8,128)S(1)}) custom-call(f32[2,1,125,2,128]{4,3,2,1,0:T(2,128)} %bitcast.11, f32[2,1,2]{2,1,0:T(1,128)S(1)} %copy-done, f32[2,1,2]{2,1,0:T(1,128)S(1)} %copy-done.1, s32[1,2]{1,0:T(1,128)S(1)} %bitcast.9, s32[1,2]{1,0:T(1,128)S(1)} %bitcast.10), custom_call_target="tpu_custom_call" | custom-call | tf_op jit(solution)/shard_map/adjoint_steps/pallas_call | solution.py:761
  40.5 0.7 %copy.9 = f32[2,1,2,125,128]{4,2,3,1,0:T(2,128)} copy(f32[2,1,2,125,128]{4,2,3,1,0:T(2,128)S(1)} %bitcast.7) | data formatting | bytes 512000
  41.2 0.6 %copy.10 = f32[8,25,128]{2,0,1:T(8,128)} copy(f32[8,25,128]{2,0,1:T(8,128)S(1)} %bitcast.8) | data formatting | bytes 204800
Async XLA Ops:
  0.6 0.7 %copy-start.1 = (f32[2,1,2]{2,1,0:T(1,128)S(1)}, f32[2,1,2]{2,1,0:T(1,128)}, u32[]{:S(2)}) copy-start(f32[2,1,2]{2,1,0:T(1,128)} %buoy_hbm.1) | copy-start | bytes 52
  0.6 0.7 %copy-start.3 = (s32[2,1]{0,1:T(1,128)S(1)}, s32[2,1]{0,1:T(1,128)}, u32[]{:S(2)}) copy-start(s32[2,1]{0,1:T(1,128)} %param.9) | copy-start | bytes 28
  0.7 0.7 %copy-start = (f32[2,1,2]{2,1,0:T(1,128)S(1)}, f32[2,1,2]{2,1,0:T(1,128)}, u32[]{:S(2)}) copy-start(f32[2,1,2]{2,1,0:T(1,128)} %bulk_hbm.1) | copy-start | bytes 52
  0.7 0.7 %copy-start.2 = (s32[2,1]{0,1:T(1,128)S(1)}, s32[2,1]{0,1:T(1,128)}, u32[]{:S(2)}) copy-start(s32[2,1]{0,1:T(1,128)} %param.8) | copy-start | bytes 28

commit v3 on v2

--- a/solution.py
+++ b/solution.py
@@ -101,6 +101,15 @@
         return jnp.where(mask, lane_roll(value, wide), lane_roll(value, -short))
     return jnp.where(mask, lane_roll(value, short), lane_roll(value, -wide))
 
+
+def hops(turn, mask):
+    return min(turn, 4 - turn) + {0: 0, 1: 1, 4: 2, 5: 1}[mask & 5]
+
+
+FAR_FIRST = sorted(
+    ((turn, mask) for turn in range(4) for mask in range(8) if turn or mask),
+    key=lambda pair: (-hops(*pair), pair[1] & 5, pair[0]),
+)
 
 VOL = 0
 FACES = 3
@@ -264,8 +273,10 @@
         copy.wait_send()
 
     def swap_start(out_ref, in_ref, send, recv, by_owner=False):
-        for delta in range(1, RANKS):
-            rank = (me + delta) % RANKS
+        for turn, mask in FAR_FIRST:
+            low = [(me // (1 << b)) % 2 for b in range(3)]
+            low = [1 - v if mask & (1 << b) else v for b, v in enumerate(low)]
+            rank = ((gx + turn) % 4) * 8 + low[2] * 4 + low[1] * 2 + low[0]
             pltpu.make_async_remote_copy(
                 src_ref=out_ref.at[(rank // 8) * 2 + rank % 2 if by_owner else rank],
                 dst_ref=in_ref.at[me],
@@ -617,8 +628,6 @@
         add_outer(update, adds, sixth)
         answer = [half * term for term in flux(INTO, own, outer)]
         put_planes(ghost.at[0], answer)
-        free = arrived_planes(step, 1)
-        outer = [free[field] + answer[field] for field in range(4)]
 
         add_floor(first, third)
         own = near_planes(first)
@@ -626,9 +635,6 @@
         put_planes(near, came)
         rates(near, ghost_rate, 1, 0)
         slopes = as_planes(ghost_rate)
-        adds = [slopes[field] + term for field, term in enumerate(flux(OUTER, outer, own))]
-        add_outer(second, adds, half)
-        add_outer(update, adds, third)
         for field, source, scale in ((0, 2, coef[VOL]), (2, 0, coef[VOL + 1])):
             inward = scale * came[source]
             for j in range(5):
@@ -639,29 +645,32 @@
                     second[field, at : at + 8, :] = second[field, at : at + 8, :] + half * term[i]
                     update[field, at : at + 8, :] = update[field, at : at + 8, :] + third * term[i]
         rates(ghost.at[0], ghost_rate, 1, GHOST)
-        slopes = as_planes(ghost_rate)
-        answer = [half * (slopes[field] + term) for field, term in enumerate(flux(INTO, own, outer))]
+        answered = as_planes(ghost_rate)
+        free = arrived_planes(step, 1)
+        outer = [free[field] + answer[field] for field in range(4)]
+        adds = [slopes[field] + term for field, term in enumerate(flux(OUTER, outer, own))]
+        add_outer(second, adds, half)
+        add_outer(update, adds, third)
+        answer = [half * (answered[field] + term) for field, term in enumerate(flux(INTO, own, outer))]
         put_planes(ghost.at[1], answer)
-        free = arrived_planes(step, 2)
-        outer = [free[field] + answer[field] for field in range(4)]
 
         add_floor(second, third)
         rates(second, rate, 5, 0)
-        own = near_planes(second)
-        adds = flux(OUTER, outer, own)
+        rates(ghost.at[1], ghost_rate, 1, GHOST)
+        answered = as_planes(ghost_rate)
         for field in range(4):
             third_in[field] = now[field] + DT * rate[field]
             update[field] = update[field] + third * rate[field]
+        own = near_planes(second)
+        early = as_planes(ghost.at[0])
+        for field in (0, 2):
+            answered[field] = answered[field] + half * (coef[INTO + 4] * early[field])
+        free = arrived_planes(step, 2)
+        outer = [free[field] + term for field, term in enumerate(as_planes(ghost.at[1]))]
+        adds = flux(OUTER, outer, own)
         add_outer(third_in, adds, DT)
         add_outer(update, adds, third)
-        rates(ghost.at[1], ghost_rate, 1, GHOST)
-        slopes = as_planes(ghost_rate)
-        early = as_planes(ghost.at[0])
-        for field in (0, 2):
-            slopes[field] = slopes[field] + half * (coef[INTO + 4] * early[field])
-        answer = [DT * (slopes[field] + term) for field, term in enumerate(flux(INTO, own, outer))]
-        free = arrived_planes(step, 3)
-        outer = [free[field] + answer[field] for field in range(4)]
+        answer = [DT * (answered[field] + term) for field, term in enumerate(flux(INTO, own, outer))]
 
         add_floor(third_in, sixth)
 
@@ -670,6 +679,8 @@
             send_floor()
 
         rates(third_in, rate, 5, 0)
+        free = arrived_planes(step, 3)
+        outer = [free[field] + answer[field] for field in range(4)]
         adds = flux(OUTER, outer, near_planes(third_in))
         for field in range(4):
             now[field] = now[field] + update[field] + sixth * rate[field]
@@ -702,13 +713,16 @@
             cell = owner * S_DEV + (to_lane // 4) % 8
             chosen[128 * at : 128 * at + 128, 128 * upper : 128 * upper + 128] = jnp.where(
                 same_field & (label == cell), 1.0, 0.0
-            )
+            ).astype(jnp.bfloat16)
     for steps in (1, 2):
         trace_copy(steps).wait_recv()
-    total = jnp.dot(
-        jnp.concatenate([tr_out[...], tr_in[0], tr_in[1]], axis=1), chosen[...],
-        precision=lax.Precision.HIGHEST, preferred_element_type=jnp.float32,
-    )
+    rest = jnp.concatenate([tr_out[...], tr_in[0], tr_in[1]], axis=1)
+    thirds = []
+    for _ in range(3):
+        thirds.append(rest.astype(jnp.bfloat16))
+        rest = rest - thirds[-1].astype(jnp.float32)
+    total = jnp.dot(jnp.concatenate(thirds, axis=0), chosen[...], preferred_element_type=jnp.float32)
+    total = total[0:32] + (total[32:64] + total[64:96])
     for upper in range(2):
         part = total[:, 128 * upper : 128 * upper + 128]
         tb_out[4 * upper : 4 * upper + 4] = swap_bits(part.reshape(4, 8, 128), 2)
@@ -758,6 +772,10 @@
     in_any = pl.BlockSpec(memory_space=pl.ANY)
     dma = pltpu.SemaphoreType.DMA
     by_node = jnp.transpose(adjoint_state, (0, 1, 3, 2, 4))
+    in_hbm = [
+        pltpu.with_memory_space_constraint(value, pltpu.HBM)
+        for value in (by_node, bulk_modulus, buoyancy, water_layers.T, surface_cell.T)
+    ]
     out, trace = pl.pallas_call(
         kernel,
         out_shape=(
@@ -791,7 +809,7 @@
             pltpu.VMEM((2, 32, 128), f32),
             pltpu.VMEM((8, 128), f32),
             pltpu.VMEM((2, 8, 128), f32),
-            pltpu.VMEM((384, 256), f32),
+            pltpu.VMEM((384, 256), jnp.bfloat16),
             pltpu.VMEM((8, 8, 128), f32),
             pltpu.VMEM((32, 8, 128), f32),
             dma((5,)),
@@ -807,10 +825,10 @@
             dma,
         ],
         compiler_params=pltpu.CompilerParams(
-            collective_id=0, has_side_effects=True, vmem_limit_bytes=54656 * 1024
+            collective_id=0, has_side_effects=True, vmem_limit_bytes=32 * 1024 * 1024
         ),
         name="adjoint_steps",
-    )(by_node, bulk_modulus, buoyancy, water_layers.T, surface_cell.T)
+    )(*in_hbm)
     return (
         jnp.transpose(out, (0, 1, 3, 2, 4)),
         jnp.transpose(trace.reshape(25, S_DEV, 128), (1, 0, 2)),

time: 41.9 us -> 39.6 us (0.945)
  Pallas kernels: 39.1 us -> 37.5 us
  local copies, waits for them, and re-layouts: 2.02 us -> 1.34 us
    pallas_call x1, Pallas kernels: 39.1 us -> 37.5 us  [shards(): pl.pallas_call(kernel, out_shape=(jax.ShapeDtypeStruct(by_node.shape, f32...]
    unnamed x10 -> x2, local copies, waits for them, and re-layouts: 2.02 us -> 1.34 us
where the time goes in v3:
time: 39.6 us; the launch traced here: 39.5 us
  Pallas kernels  37.5 us (95%)
  local copies, waits for them, and re-layouts  1.34 us (3%)
  between operations  0.64 us (2%)
    pallas_call x1, Pallas kernels, shards(): pl.pallas_call(kernel, out_shape=(jax.ShapeDtypeStruct(by_node.shape, f32...  37.5 us
    unnamed x2, local copies, waits for them, and re-layouts  1.34 us

profile of v3, /device:TPU:1, one launch (start us, length us, event | category | flops | bytes accessed | tf_op | source)
XLA Modules:
  0.0 39.5 jit_solution(13702174988068925834)
XLA Ops:
  0.6 37.5 %adjoint_steps.1 = (f32[2,1,125,2,128]{4,3,2,1,0:T(2,128)S(1)}, f32[200,128]{1,0:T(8,128)S(1)}) custom-call(f32[2,1,125,2,128]{4,3,2,1,0:T(2,128)} %bitcast.9, f32[2,1,2]{2,1,0:T(1,128)} %bulk_hbm.1, f32[2,1,2]{2,1,0:T(1,128)} %buoy_hbm.1, s32[1,2]{1,0:T(1,128)} %bitcast.10, s32[1,2]{1,0:T(1,128)} %bitcast.11), custom_call_target="tpu_custom_call" | custom-call | tf_op jit(solution)/shard_map/adjoint_steps/pallas_call | solution.py:779
  38.2 0.7 %copy.9 = f32[2,1,2,125,128]{4,2,3,1,0:T(2,128)} copy(f32[2,1,2,125,128]{4,2,3,1,0:T(2,128)S(1)} %bitcast.7) | data formatting | bytes 512000
  38.9 0.6 %copy.10 = f32[8,25,128]{2,0,1:T(8,128)} copy(f32[8,25,128]{2,0,1:T(8,128)S(1)} %bitcast.8) | data formatting | bytes 204800

commit v4 on v3

--- a/solution.py
+++ b/solution.py
@@ -127,7 +127,7 @@
 def kernel(
     state_hbm, bulk_hbm, buoy_hbm, layers_hbm, cells_hbm, out, trace,
     bulk, buoy, layers, cells,
-    staged, nat, pack_out, pack_in, back_out, back_in, state, update, rate, coef,
+    staged, nat, pack_out, pack_in, back_out, back_in, state, rate, coef,
     near, ghost, ghost_rate, face_out, face_in, floor, tr_out, tr_in, label_out, label_in, chosen, tb_out, tb_in,
     local_sem, a_send, a_recv, h_send, h_recv, t_send, t_recv, b_send, b_recv, c_send, c_recv,
 ):
@@ -590,12 +590,10 @@
         rates(now, rate, 5, 0)
         for field in range(4):
             first[field] = now[field] + half * rate[field]
-            update[field] = sixth * rate[field]
         send_planes(step, 1, near_planes(first))
         rates(first, rate, 5, 0)
         for field in range(4):
             second[field] = now[field] + half * rate[field]
-            update[field] = update[field] + third * rate[field]
         planes = near_planes(second)
         send_planes(step, 2, planes)
         put_planes(near, planes)
@@ -625,7 +623,6 @@
         own = near_planes(now)
         adds = flux(OUTER, outer, own)
         add_outer(first, adds, half)
-        add_outer(update, adds, sixth)
         answer = [half * term for term in flux(INTO, own, outer)]
         put_planes(ghost.at[0], answer)
 
@@ -643,14 +640,12 @@
                 for i in range(5):
                     at = 40 * i + 8 * j
                     second[field, at : at + 8, :] = second[field, at : at + 8, :] + half * term[i]
-                    update[field, at : at + 8, :] = update[field, at : at + 8, :] + third * term[i]
         rates(ghost.at[0], ghost_rate, 1, GHOST)
         answered = as_planes(ghost_rate)
         free = arrived_planes(step, 1)
         outer = [free[field] + answer[field] for field in range(4)]
         adds = [slopes[field] + term for field, term in enumerate(flux(OUTER, outer, own))]
         add_outer(second, adds, half)
-        add_outer(update, adds, third)
         answer = [half * (answered[field] + term) for field, term in enumerate(flux(INTO, own, outer))]
         put_planes(ghost.at[1], answer)
 
@@ -660,7 +655,6 @@
         answered = as_planes(ghost_rate)
         for field in range(4):
             third_in[field] = now[field] + DT * rate[field]
-            update[field] = update[field] + third * rate[field]
         own = near_planes(second)
         early = as_planes(ghost.at[0])
         for field in (0, 2):
@@ -669,7 +663,6 @@
         outer = [free[field] + term for field, term in enumerate(as_planes(ghost.at[1]))]
         adds = flux(OUTER, outer, own)
         add_outer(third_in, adds, DT)
-        add_outer(update, adds, third)
         answer = [DT * (answered[field] + term) for field, term in enumerate(flux(INTO, own, outer))]
 
         add_floor(third_in, sixth)
@@ -683,7 +676,8 @@
         outer = [free[field] + answer[field] for field in range(4)]
         adds = flux(OUTER, outer, near_planes(third_in))
         for field in range(4):
-            now[field] = now[field] + update[field] + sixth * rate[field]
+            inputs = (first[field] - now[field]) + 2.0 * second[field] + third_in[field]
+            now[field] = (1.0 / 3.0) * inputs + sixth * rate[field]
         add_outer(now, adds, sixth)
 
         @pl.when(step < STEPS - 1)
@@ -796,7 +790,6 @@
             pltpu.VMEM((32, 16, 128), f32),
             pltpu.VMEM((32, 16, 128), f32),
             pltpu.VMEM((4, 4, 200, 128), f32),
-            pltpu.VMEM((4, 200, 128), f32),
             pltpu.VMEM((4, 200, 128), f32),
             pltpu.VMEM((N_COEF, 8, 128), f32),
             pltpu.VMEM((4, 40, 128), f32),

time: 39.6 us -> 39.5 us (level)
  no operation moved by 1% of the time
where the time goes in v4:
time: 39.5 us; the launch traced here: 39.4 us
  Pallas kernels  37.4 us (95%)
  local copies, waits for them, and re-layouts  1.34 us (3%)
  between operations  0.64 us (2%)
    pallas_call x1, Pallas kernels, shards(): pl.pallas_call(kernel, out_shape=(jax.ShapeDtypeStruct(by_node.shape, f32...  37.4 us
    unnamed x2, local copies, waits for them, and re-layouts  1.34 us

profile of v4, /device:TPU:1, one launch (start us, length us, event | category | flops | bytes accessed | tf_op | source)
XLA Modules:
  0.0 39.4 jit_solution(4345873788930256435)
XLA Ops:
  0.6 37.4 %adjoint_steps.1 = (f32[2,1,125,2,128]{4,3,2,1,0:T(2,128)S(1)}, f32[200,128]{1,0:T(8,128)S(1)}) custom-call(f32[2,1,125,2,128]{4,3,2,1,0:T(2,128)} %bitcast.9, f32[2,1,2]{2,1,0:T(1,128)} %bulk_hbm.1, f32[2,1,2]{2,1,0:T(1,128)} %buoy_hbm.1, s32[1,2]{1,0:T(1,128)} %bitcast.10, s32[1,2]{1,0:T(1,128)} %bitcast.11), custom_call_target="tpu_custom_call" | custom-call | tf_op jit(solution)/shard_map/adjoint_steps/pallas_call | solution.py:773
  38.0 0.7 %copy.9 = f32[2,1,2,125,128]{4,2,3,1,0:T(2,128)} copy(f32[2,1,2,125,128]{4,2,3,1,0:T(2,128)S(1)} %bitcast.7) | data formatting | bytes 512000
  38.7 0.6 %copy.10 = f32[8,25,128]{2,0,1:T(8,128)} copy(f32[8,25,128]{2,0,1:T(8,128)S(1)} %bitcast.8) | data formatting | bytes 204800

commit v5 on v4

--- a/solution.py
+++ b/solution.py
@@ -128,7 +128,7 @@
     state_hbm, bulk_hbm, buoy_hbm, layers_hbm, cells_hbm, out, trace,
     bulk, buoy, layers, cells,
     staged, nat, pack_out, pack_in, back_out, back_in, state, rate, coef,
-    near, ghost, ghost_rate, face_out, face_in, floor, tr_out, tr_in, label_out, label_in, chosen, tb_out, tb_in,
+    near, ghost, ghost_rate, face_out, face_in, floor, tr_out, tr_in, label_out, label_in, chosen, tb_out, tb_in, sums_out,
     local_sem, a_send, a_recv, h_send, h_recv, t_send, t_recv, b_send, b_recv, c_send, c_recv,
 ):
     gx = lax.axis_index("gx")
@@ -137,7 +137,7 @@
     zc, y_lo = gy // 2, gy % 2
     me = gx * 8 + gz * 2 + y_lo
 
-    load = pltpu.make_async_copy(state_hbm, staged, local_sem.at[0])
+    load = pltpu.make_async_copy(state_hbm, staged.at[pl.ds(0, 2)], local_sem.at[0])
     load.start()
     small = [
         pltpu.make_async_copy(source, target, local_sem.at[1 + at])
@@ -728,12 +728,17 @@
     put_blocks(nat, swap_bits(back_in[...].reshape(32, 2, 8, 128), 5))
     elements = field_swap([nat[field, 0:125] for field in range(4)])
     for e in range(4):
-        out[e // 2, 0, :, e % 2, :] = elements[e]
+        staged[e // 2, 0, :, e % 2, :] = elements[e]
+
+    store = pltpu.make_async_copy(staged.at[pl.ds(0, 2)], out, local_sem.at[5])
+    store.start()
 
     swap_whole(*ends).wait_recv()
     sums = swap_bits(tb_in[...], 5).reshape(8, 32, 128)
     for cell in range(S_DEV):
-        trace[pl.ds(cell, 25, stride=8), :] = sums[cell, 0:25]
+        sums_out[pl.ds(cell, 25, stride=8), :] = sums[cell, 0:25]
+    store_trace = pltpu.make_async_copy(sums_out.at[pl.ds(0, 8 * 25)], trace, local_sem.at[6])
+    store_trace.start()
 
     for swap in (into, back, ends):
         swap_whole(*swap).wait_send()
@@ -759,6 +764,8 @@
         return carry
 
     lax.fori_loop(0, STEPS, drain, 0)
+    store.wait()
+    store_trace.wait()
 
 
 def shards(adjoint_state, bulk_modulus, buoyancy, water_layers, surface_cell):
@@ -777,24 +784,24 @@
             jax.ShapeDtypeStruct((S_DEV * 25, 128), f32),
         ),
         in_specs=[in_any] * 5,
-        out_specs=(pl.BlockSpec(memory_space=pltpu.VMEM),) * 2,
+        out_specs=(in_any, in_any),
         scratch_shapes=[
             pltpu.SMEM(bulk_modulus.shape, f32),
             pltpu.SMEM(buoyancy.shape, f32),
             pltpu.SMEM(water_layers.T.shape, jnp.int32),
             pltpu.SMEM(surface_cell.T.shape, jnp.int32),
-            pltpu.VMEM(by_node.shape, f32),
+            pltpu.VMEM((3,) + by_node.shape[1:], f32),
             pltpu.VMEM((4, 128, 128), f32),
             pltpu.VMEM((32, 16, 128), f32),
             pltpu.VMEM((32, 16, 128), f32),
             pltpu.VMEM((32, 16, 128), f32),
             pltpu.VMEM((32, 16, 128), f32),
-            pltpu.VMEM((4, 4, 200, 128), f32),
-            pltpu.VMEM((4, 200, 128), f32),
+            pltpu.VMEM((5, 4, 200, 128), f32),
+            pltpu.VMEM((5, 200, 128), f32),
             pltpu.VMEM((N_COEF, 8, 128), f32),
-            pltpu.VMEM((4, 40, 128), f32),
-            pltpu.VMEM((2, 4, 40, 128), f32),
-            pltpu.VMEM((4, 40, 128), f32),
+            pltpu.VMEM((5, 40, 128), f32),
+            pltpu.VMEM((3, 4, 40, 128), f32),
+            pltpu.VMEM((5, 40, 128), f32),
             pltpu.VMEM((STEPS, 2, 4, 56, 128), f32),
             pltpu.VMEM((STEPS, 2, 4, 56, 128), f32),
             pltpu.VMEM((4, 25, 128), f32),
@@ -805,7 +812,8 @@
             pltpu.VMEM((384, 256), jnp.bfloat16),
             pltpu.VMEM((8, 8, 128), f32),
             pltpu.VMEM((32, 8, 128), f32),
-            dma((5,)),
+            pltpu.VMEM((256, 128), f32),
+            dma((7,)),
             dma,
             dma,
             dma((STEPS, 2)),

time: 39.5 us -> 39.6 us (level)
  no operation moved by 1% of the time
where the time goes in v5:
time: 39.6 us; the launch traced here: 39.5 us
  Pallas kernels  37.5 us (95%)
  local copies, waits for them, and re-layouts  1.34 us (3%)
  between operations  0.64 us (2%)
    pallas_call x1, Pallas kernels, shards(): pl.pallas_call(kernel, out_shape=(jax.ShapeDtypeStruct(by_node.shape, f32...  37.5 us
    unnamed x2, local copies, waits for them, and re-layouts  1.34 us

profile of v5, /device:TPU:1, one launch (start us, length us, event | category | flops | bytes accessed | tf_op | source)
XLA Modules:
  0.0 39.5 jit_solution(17378134102457371637)
XLA Ops:
  0.6 37.5 %adjoint_steps.1 = (f32[2,1,125,2,128]{4,3,2,1,0:T(2,128)S(1)}, f32[200,128]{1,0:T(8,128)S(1)}) custom-call(f32[2,1,125,2,128]{4,3,2,1,0:T(2,128)} %bitcast.9, f32[2,1,2]{2,1,0:T(1,128)} %bulk_hbm.1, f32[2,1,2]{2,1,0:T(1,128)} %buoy_hbm.1, s32[1,2]{1,0:T(1,128)} %bitcast.10, s32[1,2]{1,0:T(1,128)} %bitcast.11), custom_call_target="tpu_custom_call" | custom-call | tf_op jit(solution)/shard_map/adjoint_steps/pallas_call | solution.py:780
  38.2 0.7 %copy.9 = f32[2,1,2,125,128]{4,2,3,1,0:T(2,128)} copy(f32[2,1,2,125,128]{4,2,3,1,0:T(2,128)S(1)} %bitcast.7) | data formatting | bytes 512000
  38.9 0.6 %copy.10 = f32[8,25,128]{2,0,1:T(8,128)} copy(f32[8,25,128]{2,0,1:T(8,128)S(1)} %bitcast.8) | data formatting | bytes 204800
